TPU v7x, 32 devices: a whole 2x2x4 slice. The times are simulated.
32 devices in a mesh: row: 2 (over core), col: 4 (over y, x), depth: 4 (over z).
Axes of the slice: x: 2, y: 2, z: 4, core: 2. Of those that a mesh axis runs over, the one named last changes fastest.
Arguments:
- tokens: bfloat16 [128, 12288], P(('col', 'depth'), 'row'), may hold values from -6 to 6
- cotangent: bfloat16 [128, 12288], P(('col', 'depth'), 'row'), may hold values from -0.375 to 0.375
- w_in: bfloat16 [12288, 24576], P('row', ('col', 'depth')), may hold values from -0.0546875 to 0.0546875
- b_in: float32 [24576], P('col'), may hold values from -4 to 4
- w_out: bfloat16 [24576, 12288], P('col', ('row', 'depth')), may hold values from -0.0390625 to 0.0390625
Outputs:
- input_grad: bfloat16 [128, 12288], P(('col', 'depth'), 'row')
- w_in_grad: bfloat16 [12288, 24576], P('row', ('col', 'depth'))
- b_in_grad: float32 [24576], P(('col', 'depth'))
- w_out_grad: bfloat16 [24576, 12288], P('col', ('row', 'depth'))
All inputs are finite; a program needn't handle non-finite values.
Results may differ from a plain program's by a relative error of at most 0.0065.
Values may be sent and summed in bfloat16 or wider, within the bound.
A program may use at most 320 MiB of HBM per device.

v0:
```python
import jax
import jax.numpy as jnp
from jax import lax
from jax.sharding import PartitionSpec as P

coef = 0.7978845608


def gelu_pair(pre):
    inner = coef * (pre + 0.044715 * pre * pre * pre)
    tanh_v = jnp.tanh(inner)
    act = 0.5 * pre * (1.0 + tanh_v)
    slope = 0.5 * (1.0 + tanh_v) + 0.5 * pre * (1.0 - tanh_v * tanh_v) * coef * (
        1.0 + 0.134145 * pre * pre
    )
    return (act, slope)


def against(left, right):
    return lax.dot_general(
        left, right, (((1,), (1,)), ((), ())), preferred_element_type=jnp.float32
    )


def shards(tokens, cotangent, w_in, b_in, w_out):
    n_rows = lax.axis_size("row")
    n_cols = lax.axis_size("col")
    n_depth = lax.axis_size("depth")
    depth_at = lax.axis_index("depth")
    tok_dev = tokens.shape[0]
    feat_cols = tokens.shape[1]
    tile_hidden = b_in.shape[0]
    quarter_h = w_in.shape[1]
    quarter_d = w_out.shape[1]
    every_x, every_g = (
        lax.all_gather(tokens, ("col", "depth"), axis=0, tiled=True),
        lax.all_gather(cotangent, ("col", "depth"), axis=0, tiled=True),
    )

    def own_copy(whole):
        shaped = whole.reshape(n_cols, n_depth, tok_dev, feat_cols)
        picked = lax.dynamic_index_in_dim(shaped, depth_at, 1, keepdims=False)
        return picked.reshape(n_cols * tok_dev, feat_cols)

    copy_x = own_copy(every_x)
    copy_g = own_copy(every_g)
    tile_in, tile_out = (
        lax.all_gather(w_in, "depth", axis=1, tiled=True),
        lax.all_gather(w_out, "depth", axis=1, tiled=True),
    )
    pre_part = jnp.dot(copy_x, tile_in, preferred_element_type=jnp.float32)
    back_part = against(copy_g, tile_out)
    pre_rows, back_rows = (
        lax.psum_scatter(pre_part, "row", scatter_dimension=0, tiled=True),
        lax.psum_scatter(back_part, "row", scatter_dimension=0, tiled=True),
    )
    pre_rows = pre_rows + b_in
    act_f, slope = gelu_pair(pre_rows)
    act = act_f.astype(jnp.bfloat16)
    grad_pre = (back_rows * slope).astype(jnp.bfloat16)
    rows_here = pre_rows.shape[0]
    per_row = rows_here // tok_dev
    all_act, all_grad = (
        lax.all_gather(act, ("row", "depth"), axis=0, tiled=True),
        lax.all_gather(grad_pre, ("row", "depth"), axis=0, tiled=True),
    )
    grid_grad = all_grad.reshape(n_rows, n_depth, rows_here, tile_hidden)
    copy_grad = lax.dynamic_index_in_dim(grid_grad, depth_at, 1, keepdims=False).reshape(
        n_rows * rows_here, tile_hidden
    )
    quarter_grad = lax.dynamic_slice_in_dim(all_grad, depth_at * quarter_h, quarter_h, 1)
    tok_grid = every_x.reshape(n_rows, per_row, n_depth, tok_dev, feat_cols)
    grad_grid = quarter_grad.reshape(n_rows, n_depth, per_row, tok_dev, quarter_h)
    w_in_sum = jnp.einsum(
        "rcdtk,rdctn->kn", tok_grid, grad_grid, preferred_element_type=jnp.float32
    )
    quarter_g = lax.dynamic_slice_in_dim(every_g, depth_at * quarter_d, quarter_d, 1)
    cot_grid = quarter_g.reshape(n_rows, per_row, n_depth, tok_dev, quarter_d)
    act_grid = all_act.reshape(n_rows, n_depth, per_row, tok_dev, tile_hidden)
    w_out_sum = jnp.einsum(
        "rdctk,rcdtn->kn", act_grid, cot_grid, preferred_element_type=jnp.float32
    )
    b_in_grad = jnp.sum(quarter_grad.astype(jnp.float32), axis=0)
    input_part = against(copy_grad, tile_in)
    input_grad = lax.psum_scatter(input_part, "col", scatter_dimension=0, tiled=True).astype(
        jnp.bfloat16
    )
    return (input_grad, w_in_sum.astype(jnp.bfloat16), b_in_grad, w_out_sum.astype(jnp.bfloat16))


def solution(mesh):
    return jax.shard_map(
        shards,
        mesh=mesh,
        in_specs=(
            P(("col", "depth"), "row"),
            P(("col", "depth"), "row"),
            P("row", ("col", "depth")),
            P("col"),
            P("col", ("row", "depth")),
        ),
        out_specs=(
            P(("col", "depth"), "row"),
            P("row", ("col", "depth")),
            P(("col", "depth")),
            P("col", ("row", "depth")),
        ),
        check_vma=False,
    )
```

profile of v0, /device:TPU:0, one launch (start us, length us, event | category | flops | bytes accessed | tf_op | source)
XLA Modules:
  0.0 2811.8 jit_solution(11370244686730412323)
XLA Ops:
  7.2 0.7 all-gather.7.cloned.1.call-update
  7.9 0.7 all-gather.9.cloned.1.call-update
  8.7 0.7 all-gather.11.cloned.1.call-update
  9.4 0.5 all-gather.13.cloned.1.call-update
  10.0 61.5 %all-gather.7.cloned.1.call-done = bf16[128,6144]{1,0:T(8,128)(2,1)} async-done(((bf16[8,6144]{1,0:T(8,128)(2,1)}), bf16[128,6144]{1,0:T(8,128)(2,1)}) %all-gather.7.cloned.1.call-update) | async-done | bytes 1572880 | tf_op jit(solution)/shard_map/all_gather | solution.py:37
  71.5 1249.3 %all-gather.9.cloned.1.call-done = bf16[6144,6144]{1,0:T(8,128)(2,1)} async-done(((bf16[6144,1536]{1,0:T(8,128)(2,1)}), bf16[6144,6144]{1,0:T(8,128)(2,1)}) %all-gather.9.cloned.1.call-update) | async-done | bytes 75497488 | tf_op jit(solution)/shard_map/all_gather | solution.py:49
  1320.8 30.1 %fusion.12 = f32[32,6144]{1,0:T(8,128)} fusion(bf16[6144,6144]{1,0:T(8,128)(2,1)} %all-gather.9.cloned.1.call-done, bf16[4,4,8,6144]{3,2,1,0:T(8,128)(2,1)} %bitcast.32, s32[]{:T(128)S(6)} %select_n.11), kind=kOutput, calls=%fused_computation.17 | convolution fusion | flops 2415919104 | bytes 76677120 | tf_op jit(solution)/shard_map/dot_general | solution.py:20
  1351.0 28.9 %all-gather.11.cloned.1.call-done = bf16[128,6144]{1,0:T(8,128)(2,1)} async-done(((bf16[8,6144]{1,0:T(8,128)(2,1)}), bf16[128,6144]{1,0:T(8,128)(2,1)}) %all-gather.11.cloned.1.call-update) | async-done | bytes 1572880 | tf_op jit(solution)/shard_map/all_gather | solution.py:36
  1379.9 1249.2 %all-gather.13.cloned.1.call-done = bf16[6144,6144]{1,0:T(8,128)(2,1)} async-done(((bf16[6144,1536]{1,0:T(8,128)(2,1)}), bf16[6144,6144]{1,0:T(8,128)(2,1)}) %all-gather.13.cloned.1.call-update) | async-done | bytes 75497488 | tf_op jit(solution)/shard_map/all_gather | solution.py:48
  2629.1 28.7 %fusion.10 = f32[32,6144]{1,0:T(8,128)} fusion(bf16[6144,6144]{1,0:T(8,128)(2,1)} %all-gather.13.cloned.1.call-done, bf16[4,4,8,6144]{3,2,1,0:T(8,128)(2,1)} %bitcast.36, s32[]{:T(128)S(6)} %select_n.11), kind=kOutput, calls=%fused_computation.15 | convolution fusion | flops 2415919104 | bytes 76677120 | tf_op jit(solution)/shard_map/dot_general | solution.py:51
  2657.9 6.5 reduce-scatter.5.cloned.1.call-done
  2664.4 2.1 multiply_convert_fusion
  2666.6 0.2 all-gather.17.cloned.1.call-start
  2666.8 0.6 dynamic-slice
  2668.1 1.0 constant_dynamic-slice_fusion
  2669.1 23.8 all-gather.15.cloned.1.call-done
  2693.0 1.0 constant_dynamic-slice_fusion.2
  2694.0 1.7 convert_reduce_fusion
  2695.7 9.5 fusion
  2705.2 29.5 %fusion.20 = f32[32,6144]{1,0:T(8,128)S(1)} fusion(bf16[32,6144]{1,0:T(8,128)(2,1)S(1)} %bitcast.31, bf16[6144,6144]{1,0:T(8,128)(2,1)} %all-gather.13.cloned.1.call-done), kind=kOutput, calls=%fused_computation.30 | convolution fusion | flops 2415919104 | bytes 76677120 | tf_op jit(solution)/shard_map/dot_general | solution.py:20
  2734.6 24.6 copy.20
  2759.2 34.2 %all-reduce.2 = bf16[32,6144]{1,0:T(8,128)(2,1)S(1)} all-reduce(f32[32,6144]{1,0:T(8,128)S(1)} %fusion.20), channel_id=4, replica_groups=mesh['row'=2,'col'=4,'depth'=4] {'col'}, use_global_device_ids=true, to_apply=%region_2.3.clone | all-reduce | flops 196608 | bytes 1179648
  2793.4 0.7 dynamic-slice_convert_fusion
  2794.1 10.9 bitcast_convert_fusion
  (19 shorter events, 0.4 us)
Async XLA Ops:
  7.2 64.3 %all-gather.7.cloned.1.call-start = ((), (), s32[]{:S(2)}) async-start(), calls=%async_computation.2 | async-start | bytes 1671168 | tf_op jit(solution)/shard_map/all_gather | solution.py:37
  7.9 1312.9 %all-gather.9.cloned.1.call-start = ((), (), s32[]{:S(2)}) async-start(), calls=%async_computation.3 | async-start | bytes 94371840 | tf_op jit(solution)/shard_map/all_gather | solution.py:49
  8.6 1371.3 %all-gather.11.cloned.1.call-start = ((), (), s32[]{:S(2)}) async-start(), calls=%async_computation.5 | async-start | bytes 1671168 | tf_op jit(solution)/shard_map/all_gather | solution.py:36
  9.4 2619.7 %all-gather.13.cloned.1.call-start = ((), (), s32[]{:S(2)}) async-start(), calls=%async_computation.6 | async-start | bytes 94371840 | tf_op jit(solution)/shard_map/all_gather | solution.py:48
  10.0 2647.9 %reduce-scatter.3.cloned.1.call-start = ((), (), s32[]{:S(2)}) async-start(), calls=%async_computation.4 | async-start | bytes 1179648 | tf_op jit(solution)/shard_map/reduce_scatter | solution.py:55
  1350.9 1313.5 %reduce-scatter.5.cloned.1.call-start = ((), (), s32[]{:S(2)}) async-start(), calls=%async_computation.7 | async-start | bytes 1179648 | tf_op jit(solution)/shard_map/reduce_scatter | solution.py:54
  2629.1 35.4 %copy-start.1 = (f32[6144]{0:T(1024)S(1)}, f32[6144]{0:T(1024)}, u32[]{:S(2)}) copy-start(f32[6144]{0:T(1024)} %param.8) | copy-start | bytes 73732
  2629.1 37.8 %copy-start.2 = (u32[32]{0:T(128)S(1)}, u32[32]{0:T(128)}, u32[]{:S(2)}) copy-start(u32[32]{0:T(128)} %constant.37) | copy-start | bytes 388
  2629.1 66.6 %copy-start = (bf16[128,6144]{1,0:T(8,128)(2,1)S(1)}, bf16[128,6144]{1,0:T(8,128)(2,1)}, u32[]{:S(2)}) copy-start(bf16[128,6144]{1,0:T(8,128)(2,1)} %all-gather.11.cloned.1.call-done) | copy-start | bytes 4718596
  2657.8 35.1 %all-gather.15.cloned.1.call-start = ((), (), s32[]{:S(2)}) async-start(), calls=%async_computation.8 | async-start | bytes 1769472 | tf_op jit(solution)/shard_map/all_gather | solution.py:65
  2666.6 127.5 %all-gather.17.cloned.1.call-start = ((), (), s32[]{:S(2)}) async-start(), calls=%async_computation.9 | async-start | bytes 1769472 | tf_op jit(solution)/shard_map/all_gather | solution.py:64
Sparse Core Ops, SparseCore 0:
  10.8 60.5 all-gather.6
  73.1 1247.6 all-gather.8
  1323.6 56.2 all-gather.10
  1381.3 1247.6 all-gather.12
  2631.7 6.4 reduce-scatter.2
  2658.0 6.4 reduce-scatter.4
  2666.7 26.1 all-gather.14
  2694.6 24.5 all-gather.16
where the time goes:
time: 2810 us
  waiting for transfers between devices  2620 us (93%)
  matrix products  109 us (4%)
  blocking collectives  34.2 us (1%)
    all_gather x1, waiting for transfers between devices, shards(): lax.all_gather(w_out, 'depth', axis=1, tiled=True)  1250 us
    all_gather x1, waiting for transfers between devices, shards(): lax.all_gather(w_in, 'depth', axis=1, tiled=True)  1250 us
    all_gather x1, waiting for transfers between devices, shards(): lax.all_gather(cotangent, ('col', 'depth'), axis=0, tiled=True)  61.5 us
    dot_general x2, matrix products, against(): lax.dot_general(left, right, (((1,), (1,)), ((), ())), preferred_element_...  59.6 us
  transfers between devices with their start and end apart: 8, of which 6 were waited for; matrix products, arithmetic and copies ran while one was open for 5% of the time, Pallas kernels for 0%

commit v1 on v0

v1 whole, which is shorter than its diff:
```python
import jax
import jax.numpy as jnp
from jax import lax
from jax.sharding import PartitionSpec as P

coef = 0.7978845608


def gelu_pair(pre):
    inner = coef * (pre + 0.044715 * pre * pre * pre)
    tanh_v = jnp.tanh(inner)
    act = 0.5 * pre * (1.0 + tanh_v)
    slope = 0.5 * (1.0 + tanh_v) + 0.5 * pre * (1.0 - tanh_v * tanh_v) * coef * (
        1.0 + 0.134145 * pre * pre
    )
    return (act, slope)


def against(left, right):
    return lax.dot_general(
        left, right, (((1,), (1,)), ((), ())), preferred_element_type=jnp.float32
    )


def shards(tokens, cotangent, w_in, b_in, w_out):
    depth_at = lax.axis_index("depth")
    quarter_h = w_in.shape[1]
    every_x = lax.all_gather(tokens, ("col", "depth"), axis=0, tiled=True)
    part_g = lax.all_to_all(cotangent, "depth", split_axis=1, concat_axis=0, tiled=True)
    quarter_g = lax.all_gather(part_g, "col", axis=0, tiled=True)
    back_part = against(quarter_g, w_out)
    back_half = lax.psum_scatter(back_part, "row", scatter_dimension=0, tiled=True)
    back_rows = lax.psum_scatter(back_half, "depth", scatter_dimension=1, tiled=True)
    pre_part = jnp.dot(every_x, w_in, preferred_element_type=jnp.float32)
    pre_rows = lax.psum_scatter(pre_part, "row", scatter_dimension=0, tiled=True)
    pre_rows = pre_rows + lax.dynamic_slice_in_dim(b_in, depth_at * quarter_h, quarter_h, 0)
    act_f, slope = gelu_pair(pre_rows)
    act = act_f.astype(jnp.bfloat16)
    grad_pre = (back_rows * slope).astype(jnp.bfloat16)
    quarter_grad = lax.all_gather(grad_pre, "row", axis=0, tiled=True)
    input_part = against(quarter_grad, w_in)
    input_grad = lax.psum_scatter(
        input_part, ("col", "depth"), scatter_dimension=0, tiled=True
    ).astype(jnp.bfloat16)
    act_half = lax.all_gather(act, "depth", axis=1, tiled=True)
    all_act = lax.all_gather(act_half, "row", axis=0, tiled=True)
    over_tokens = (((0,), (0,)), ((), ()))
    w_in_sum = lax.dot_general(
        every_x, quarter_grad, over_tokens, preferred_element_type=jnp.float32
    )
    w_out_sum = lax.dot_general(
        all_act, quarter_g, over_tokens, preferred_element_type=jnp.float32
    )
    b_in_grad = jnp.sum(quarter_grad.astype(jnp.float32), axis=0)
    return (input_grad, w_in_sum.astype(jnp.bfloat16), b_in_grad, w_out_sum.astype(jnp.bfloat16))


def solution(mesh):
    return jax.shard_map(
        shards,
        mesh=mesh,
        in_specs=(
            P(("col", "depth"), "row"),
            P(("col", "depth"), "row"),
            P("row", ("col", "depth")),
            P("col"),
            P("col", ("row", "depth")),
        ),
        out_specs=(
            P(("col", "depth"), "row"),
            P("row", ("col", "depth")),
            P(("col", "depth")),
            P("col", ("row", "depth")),
        ),
        check_vma=False,
    )
```

time: 2810 us -> 305 us (0.11)
  waiting for transfers between devices: 2620 us -> 155 us
  matrix products: 109 us -> 59.8 us
    all_gather x6 -> x2, waiting for transfers between devices: 2610 us -> 26.6 us  [the longest x1 26.6 us: shards(): every_x = lax.all_gather(tokens, ('col', 'depth'), axis=0, tiled=True)]
    reduce_scatter x0 -> x2, waiting for transfers between devices: none -> 122 us  [the longest x1 83.2 us: shards(): lax.psum_scatter(input_part, ('col', 'depth'), scatter_dimension=0, tiled...]
    unnamed x1 -> x0, blocking collectives: 34.2 us -> none
    all_gather x0 -> x3, blocking collectives: none -> 31.4 us  [the longest x1 18.5 us: shards(): act_half = lax.all_gather(act, 'depth', axis=1, tiled=True)]
    dot_general x2, matrix products: 59.6 us -> 29 us  [against(): lax.dot_general(left, right, (((1,), (1,)), ((), ())), preferred_element_...]
  transfers between devices with their start and end apart: 8 -> 6, of which waited for: 6 -> 4; matrix products, arithmetic and copies ran while one was open for 5% -> 28% of each run, Pallas kernels for 0% -> 0%
where the time goes in v1:
time: 305 us; the launch traced here: 304 us
  waiting for transfers between devices  155 us (51%)
  matrix products  59.8 us (20%)
  blocking collectives  43.6 us (14%)
  local copies, waits for them, and re-layouts  25.4 us (8%)
  between operations  15.7 us (5%)
  other arithmetic  3.64 us (1%)
    reduce_scatter x1, waiting for transfers between devices, shards(): lax.psum_scatter(input_part, ('col', 'depth'), scatter_dimension=0, tiled...  83.2 us
    reduce_scatter x1, waiting for transfers between devices, shards(): lax.psum_scatter(back_half, 'depth', scatter_dimension=1, tiled=True)  38.6 us
    dot_general x2, matrix products, against(): lax.dot_general(left, right, (((1,), (1,)), ((), ())), preferred_element_...  29 us
    all_gather x1, waiting for transfers between devices, shards(): every_x = lax.all_gather(tokens, ('col', 'depth'), axis=0, tiled=True)  26.6 us
    unnamed x3, local copies, waits for them, and re-layouts  24.6 us
    all_gather x1, blocking collectives, shards(): act_half = lax.all_gather(act, 'depth', axis=1, tiled=True)  18.5 us
    all_to_all x1, blocking collectives, shards(): lax.all_to_all(cotangent, 'depth', split_axis=1, concat_axis=0, tiled=True)  12.2 us
    dot_general x1, matrix products, shards(): lax.dot_general(all_act, quarter_g, over_tokens, preferred_element_type=j...  10.9 us
  transfers between devices with their start and end apart: 6, of which 4 were waited for; matrix products, arithmetic and copies ran while one was open for 28% of the time, Pallas kernels for 0%

profile of v1, /device:TPU:0, one launch (start us, length us, event | category | flops | bytes accessed | tf_op | source)
XLA Modules:
  0.0 303.7 jit_solution(11331369475229918564)
XLA Ops:
  8.0 0.7 all-gather.3.cloned.1.call-update
  8.7 0.0 reduce-scatter.5.cloned.1.call-start
  8.8 12.2 %all_to_all.19 = bf16[8,4,1536]{2,0,1:T(8,128)(2,1)S(1)} all-to-all(bf16[8,4,1536]{2,0,1:T(8,128)(2,1)} %bitcast.17), channel_id=1, replica_groups=mesh['row'=2,'col'=4,'depth'=4] {'depth'}, dimensions={1} | all-to-all | bytes 196608 | tf_op jit(solution)/shard_map/all_to_all | solution.py:29
  20.9 10.6 %all_gather.15 = bf16[128,1536]{1,0:T(8,128)(2,1)S(1)} all-gather(bf16[32,1536]{1,0:T(8,128)(2,1)S(1)} %bitcast.16), channel_id=1, replica_groups=mesh['row'=2,'col'=4,'depth'=4] {'col'}, dimensions={0}, use_global_device_ids=true | all-gather | bytes 491520 | tf_op jit(solution)/shard_map/all_gather | solution.py:30
  31.6 14.1 %fusion.8 = f32[128,6144]{1,0:T(8,128)} fusion(bf16[128,1536]{1,0:T(8,128)(2,1)S(1)} %all_gather.15, bf16[6144,1536]{1,0:T(8,128)(2,1)} %param.9), kind=kOutput, calls=%fused_computation.14 | convolution fusion | flops 2415919104 | bytes 22413312 | tf_op jit(solution)/shard_map/dot_general | solution.py:20
  45.7 0.0 reduce-scatter.9.cloned.1.call-start
  45.7 26.6 %all-gather.3.cloned.1.call-done = bf16[128,6144]{1,0:T(8,128)(2,1)} async-done(((bf16[8,6144]{1,0:T(8,128)(2,1)}), bf16[128,6144]{1,0:T(8,128)(2,1)}) %all-gather.3.cloned.1.call-update) | async-done | bytes 1572880 | tf_op jit(solution)/shard_map/all_gather | solution.py:28
  72.3 10.3 %fusion.9 = f32[128,1536]{1,0:T(8,128)} fusion(bf16[128,6144]{1,0:T(8,128)(2,1)} %all-gather.3.cloned.1.call-done, bf16[6144,1536]{1,0:T(8,128)(2,1)} %param.7), kind=kOutput, calls=%fused_computation.15 | convolution fusion | flops 2415919104 | bytes 21233664 | tf_op jit(solution)/shard_map/dot_general | solution.py:34
  82.7 0.0 reduce-scatter.7.cloned.1.call-start
  82.8 0.5 reduce-scatter.7.cloned.1.call-update
  83.3 0.8 dynamic_slice.3
  84.1 5.6 %reduce-scatter.9.cloned.1.call-done = f32[64,1536]{1,0:T(8,128)} async-done(((f32[128,1536]{1,0:T(8,128)}), f32[64,1536]{1,0:T(8,128)}) %reduce-scatter.9.cloned.1.call-update) | async-done | bytes 393232 | tf_op jit(solution)/shard_map/reduce_scatter | solution.py:35
  89.7 38.6 %reduce-scatter.7.cloned.1.call-done = f32[64,1536]{1,0:T(8,128)} async-done(((f32[64,6144]{1,0:T(8,128)}), f32[64,1536]{1,0:T(8,128)}) %reduce-scatter.7.cloned.1.call-update) | async-done | bytes 393232 | tf_op jit(solution)/shard_map/reduce_scatter | solution.py:33
  128.4 1.4 multiply_convert_fusion
  129.8 18.5 %all_gather.18 = bf16[64,6144]{1,0:T(8,128)(2,1)} all-gather(bf16[64,1536]{1,0:T(8,128)(2,1)S(1)} %get-tuple-element.8), channel_id=1, replica_groups=mesh['row'=2,'col'=4,'depth'=4] {'depth'}, dimensions={1}, use_global_device_ids=true | all-gather | bytes 983040 | tf_op jit(solution)/shard_map/all_gather | solution.py:45
  148.3 0.0 reduce-scatter.11.cloned.1.call-start
  148.4 2.3 all_gather.17
  150.6 15.0 %fusion.10 = f32[128,6144]{1,0:T(8,128)} fusion(bf16[128,1536]{1,0:T(8,128)(2,1)S(1)} %all_gather.17, bf16[6144,1536]{1,0:T(8,128)(2,1)} %param.7), kind=kOutput, calls=%fused_computation.16 | convolution fusion | flops 2415919104 | bytes 22413312 | tf_op jit(solution)/shard_map/dot_general | solution.py:20
  165.6 9.5 %fusion = bf16[6144,1536]{0,1:T(8,128)(2,1)} fusion(bf16[128,1536]{1,0:T(8,128)(2,1)S(1)} %all_gather.17, bf16[128,6144]{1,0:T(8,128)(2,1)S(1)} %copy-done), kind=kOutput, calls=%fused_computation.2 | convolution fusion | flops 2425356288 | bytes 20840448 | tf_op jit(solution)/shard_map/dot_general | solution.py:48
  175.1 24.6 %copy.9 = bf16[6144,1536]{1,0:T(8,128)(2,1)} copy(bf16[6144,1536]{0,1:T(8,128)(2,1)} %fusion) | data formatting | bytes 37748736
  199.8 0.7 convert_reduce_fusion
  200.5 10.9 %convolution_convert_fusion = bf16[6144,1536]{1,0:T(8,128)(2,1)} fusion(bf16[128,6144]{1,0:T(8,128)(2,1)} %all-gather.5.cloned.1.call-done, bf16[128,1536]{1,0:T(8,128)(2,1)S(1)} %all_gather.15), kind=kOutput, calls=%fused_computation | convolution fusion | flops 2425356288 | bytes 20840448 | tf_op jit(solution)/shard_map/dot_general | solution.py:51
  211.4 83.2 %reduce-scatter.11.cloned.1.call-done = f32[8,6144]{1,0:T(8,128)} async-done(((f32[128,6144]{1,0:T(8,128)}), f32[8,6144]{1,0:T(8,128)}) %reduce-scatter.11.cloned.1.call-update) | async-done | bytes 196624 | tf_op jit(solution)/shard_map/reduce_scatter | solution.py:42
  294.5 1.6 convert_element_type.22
  (10 shorter events, 0.2 us)
Async XLA Ops:
  8.0 64.3 %all-gather.3.cloned.1.call-start = ((), (), s32[]{:S(2)}) async-start(), calls=%async_computation.7 | async-start | bytes 1671168 | tf_op jit(solution)/shard_map/all_gather | solution.py:28
  8.7 74.0 %reduce-scatter.5.cloned.1.call-start = ((), (), s32[]{:S(2)}) async-start(), calls=%async_computation.5 | async-start | bytes 4718592 | tf_op jit(solution)/shard_map/reduce_scatter | solution.py:32
  45.7 44.1 %reduce-scatter.9.cloned.1.call-start = ((), (), s32[]{:S(2)}) async-start(), calls=%async_computation.8 | async-start | bytes 1179648 | tf_op jit(solution)/shard_map/reduce_scatter | solution.py:35
  82.7 45.7 %reduce-scatter.7.cloned.1.call-start = ((), (), s32[]{:S(2)}) async-start(), calls=%async_computation.6 | async-start | bytes 1966080 | tf_op jit(solution)/shard_map/reduce_scatter | solution.py:33
  83.3 117.2 %all-gather.5.cloned.1.call-start = ((), (), s32[]{:S(2)}) async-start(), calls=%async_computation.10 | async-start | bytes 2359296 | tf_op jit(solution)/shard_map/all_gather | solution.py:46
  148.3 146.2 %reduce-scatter.11.cloned.1.call-start = ((), (), s32[]{:S(2)}) async-start(), calls=%async_computation.9 | async-start | bytes 3342336 | tf_op jit(solution)/shard_map/reduce_scatter | solution.py:42
  150.6 15.0 %copy-start = (bf16[128,6144]{1,0:T(8,128)(2,1)S(1)}, bf16[128,6144]{1,0:T(8,128)(2,1)}, u32[]{:S(2)}) copy-start(bf16[128,6144]{1,0:T(8,128)(2,1)} %all-gather.3.cloned.1.call-done) | copy-start | bytes 4718596
Sparse Core Ops, SparseCore 0:
  11.7 60.5 all-gather.2
  165.7 128.7 reduce-scatter.10
Sparse Core Ops, SparseCore 1:
  45.8 8.5 reduce-scatter.4
  82.8 6.9 reduce-scatter.8
  91.9 36.4 reduce-scatter.6
  148.4 8.4 all-gather.4

commit v2 on v1

v2 whole, which is shorter than its diff:
```python
import functools

import jax
import jax.numpy as jnp
from jax import lax
from jax.experimental import pallas as pl
from jax.experimental.pallas import tpu as pltpu
from jax.sharding import PartitionSpec as P

coef = 0.7978845608
MESH = pl.DeviceIdType.MESH
F32 = jnp.float32
BF16 = jnp.bfloat16
N_CHUNK = 4


def gelu_pair(pre):
    inner = coef * (pre + 0.044715 * pre * pre * pre)
    tanh_v = jnp.tanh(inner)
    act = 0.5 * pre * (1.0 + tanh_v)
    slope = 0.5 * (1.0 + tanh_v) + 0.5 * pre * (1.0 - tanh_v * tanh_v) * coef * (
        1.0 + 0.134145 * pre * pre
    )
    return (act, slope)


def against(left, right):
    return lax.dot_general(left, right, (((1,), (1,)), ((), ())), preferred_element_type=F32)


def over_tokens(left, right):
    return lax.dot_general(left, right, (((0,), (0,)), ((), ())), preferred_element_type=F32)


def block_of(size, largest=512):
    for block in (512, 384, 256, 128):
        if block <= largest and size % block == 0:
            return block
    return size


def cols_at(i, block):
    return pl.ds(pl.multiple_of(i * block, block), block)


def exchange_kernel(
    R, C, Z,
    tok_ref, cot_ref, w_in_hbm, b_ref, w_out_hbm,
    x_out, g_out, grad_out, act_out, bias_out, in_out,
    w_in_v, w_out_v, x_all, g_all, pre_part, pre_recv, back_part, back_recv,
    back_send, back_depth, act_all, grad_all, col_send, col_recv, dep_send, dep_recv,
    w_sem, x_s, x_r, g_s, g_r, pre_s, pre_r, br_s, br_r, bd_s, bd_r,
    act_s, act_r, grad_s, grad_r, col_s, col_r, dep_s, dep_r,
):
    row, col, dep = lax.axis_index("row"), lax.axis_index("col"), lax.axis_index("depth")
    size = {"row": R, "col": C, "depth": Z}
    here = {"row": row, "col": col, "depth": dep}

    def peer(axis, off):
        return lax.rem(here[axis] + off, size[axis])

    def source(axis, off):
        return lax.rem(here[axis] + size[axis] - off, size[axis])

    pending = []

    def send(axis, off, src, dst, s, r):
        copy = pltpu.make_async_remote_copy(
            src_ref=src, dst_ref=dst, send_sem=s, recv_sem=r,
            device_id={axis: peer(axis, off)}, device_id_type=MESH,
        )
        copy.start()
        pending.append(copy)
        return copy

    load_out = pltpu.make_async_copy(w_out_hbm, w_out_v, w_sem.at[0])
    load_in = pltpu.make_async_copy(w_in_hbm, w_in_v, w_sem.at[1])
    load_out.start()
    load_in.start()

    barrier = pltpu.get_barrier_semaphore()
    for axis in ("row", "col", "depth"):
        for off in range(1, size[axis]):
            pl.semaphore_signal(
                barrier, inc=1, device_id={axis: peer(axis, off)}, device_id_type=MESH
            )
    pl.semaphore_wait(barrier, R + C + Z - 3)

    own = col * Z + dep

    g_dep = {}
    x_dep = {}
    g_col = []
    x_col = []
    for off in range(1, Z):
        g_dep[off] = send("depth", off, cot_ref.at[peer("depth", off)], g_all.at[own],
                          g_s.at[off, 0], g_r.at[off, 0])
    for off in range(1, C):
        g_col.append(send("col", off, cot_ref.at[dep], g_all.at[own], g_s.at[0, off], g_r.at[0, off]))
    for off in range(1, Z):
        x_dep[off] = send("depth", off, tok_ref, x_all.at[own], x_s.at[off, 0], x_r.at[off, 0])
    for off in range(1, C):
        x_col.append(send("col", off, tok_ref, x_all.at[own], x_s.at[0, off], x_r.at[0, off]))
    g_all[own] = cot_ref[dep]
    x_all[own] = tok_ref[...]
    for off in range(1, Z):
        g_dep[off].wait_recv()
        at = col * Z + source("depth", off)
        for co in range(1, C):
            g_col.append(send("col", co, g_all.at[at], g_all.at[at], g_s.at[off, co], g_r.at[off, co]))
    for off in range(1, Z):
        x_dep[off].wait_recv()
        at = col * Z + source("depth", off)
        for co in range(1, C):
            x_col.append(send("col", co, x_all.at[at], x_all.at[at], x_s.at[off, co], x_r.at[off, co]))

    def assemble(blocks, whole):
        def pair(i, carry):
            both = jnp.concatenate(
                [blocks[2 * i].astype(F32), blocks[2 * i + 1].astype(F32)], axis=0
            )
            whole[pl.ds(pl.multiple_of(16 * i, 16), 16), :] = both.astype(BF16)
            return carry

        lax.fori_loop(0, C * Z // 2, pair, 0)

    for copy in g_col:
        copy.wait_recv()
    assemble(g_all, g_out)
    load_out.wait()
    n_half, n_hid = pre_part.shape[1], pre_part.shape[2]
    block_h = block_of(n_hid)
    back_row = []
    for d in range(Z):
        def back_step(j, carry, d=d):
            at = pl.ds(pl.multiple_of(d * n_hid + j * block_h, block_h), block_h)
            part = against(g_out[...], w_out_v[at, :])
            back_part[:, d, :, cols_at(j, block_h)] = part.reshape(R, n_half, block_h)
            return carry

        lax.fori_loop(0, n_hid // block_h, back_step, 0)
        for off in range(1, R):
            back_row.append(send("row", off, back_part.at[peer("row", off), d], back_recv.at[off - 1, d],
                                 br_s.at[off - 1, d], br_r.at[off - 1, d]))
    for copy in back_row:
        copy.wait_recv()

    def back_sum(d):
        total = back_part[row, d]
        for off in range(1, R):
            total = total + back_recv[off - 1, d]
        return total

    back_dep = []
    for off in range(1, Z):
        d = peer("depth", off)
        back_send[off] = back_sum(d).astype(BF16)
        back_dep.append(send("depth", off, back_send.at[off], back_depth.at[off], bd_s.at[off], bd_r.at[off]))

    for copy in x_col:
        copy.wait_recv()
    assemble(x_all, x_out)
    load_in.wait()
    block_p = block_of(n_hid, 256)

    def pre_step(j, carry):
        part = jnp.dot(x_out[...], w_in_v[:, cols_at(j, block_p)], preferred_element_type=F32)
        pre_part[:, :, cols_at(j, block_p)] = part.reshape(R, n_half, block_p)
        return carry

    lax.fori_loop(0, n_hid // block_p, pre_step, 0)
    pre_row = [
        send("row", off, pre_part.at[peer("row", off)], pre_recv.at[off - 1],
             pre_s.at[off - 1], pre_r.at[off - 1])
        for off in range(1, R)
    ]
    for copy in pre_row:
        copy.wait_recv()
    for copy in back_dep:
        copy.wait_recv()
    pre = pre_part[row] + b_ref[...]
    for off in range(1, R):
        pre = pre + pre_recv[off - 1]
    back = back_sum(dep)
    for off in range(1, Z):
        back = back + back_depth[off].astype(F32)
    act, slope = gelu_pair(pre)
    grad_all[row] = (back * slope).astype(BF16)
    act_all[dep, row] = act.astype(BF16)
    grad_row = [
        send("row", off, grad_all.at[row], grad_all.at[row], grad_s.at[off], grad_r.at[off])
        for off in range(1, R)
    ]
    act_dep = {
        off: send("depth", off, act_all.at[dep, row], act_all.at[dep, row],
                  act_s.at[off, 0], act_r.at[off, 0])
        for off in range(1, Z)
    }
    act_row = [
        send("row", off, act_all.at[dep, row], act_all.at[dep, row],
             act_s.at[0, off], act_r.at[0, off])
        for off in range(1, R)
    ]
    for copy in grad_row:
        copy.wait_recv()
    grad_out[...] = grad_all[...].reshape(R * n_half, n_hid)

    n_tok = dep_send.shape[2]
    chunk = col_send.shape[3]
    block_f = block_of(chunk)
    from_col = []
    for k in range(N_CHUNK):
        def in_step(j, carry, k=k):
            at = pl.ds(pl.multiple_of(k * chunk + j * block_f, block_f), block_f)
            part = against(grad_out[...], w_in_v[at, :])
            col_send[k, :, :, cols_at(j, block_f)] = part.astype(BF16).reshape(C, Z * n_tok, block_f)
            return carry

        lax.fori_loop(0, chunk // block_f, in_step, 0)
        from_col.append([
            send("col", off, col_send.at[k, peer("col", off)], col_recv.at[k, off],
                 col_s.at[k, off], col_r.at[k, off])
            for off in range(1, C)
        ])
    bias_out[...] = jnp.sum(grad_out[...].astype(F32), axis=0, keepdims=True)
    for off in range(1, Z):
        act_dep[off].wait_recv()
        at = source("depth", off)
        for ro in range(1, R):
            act_row.append(send("row", ro, act_all.at[at, row], act_all.at[at, row],
                                act_s.at[off, ro], act_r.at[off, ro]))
    from_dep = []
    for k in range(N_CHUNK):
        for copy in from_col[k]:
            copy.wait_recv()
        total = col_send[k, col].astype(F32)
        for off in range(1, C):
            total = total + col_recv[k, off].astype(F32)
        for d in range(Z):
            dep_send[k, d] = total[d * n_tok:(d + 1) * n_tok, :].astype(BF16)
        from_dep.append([
            send("depth", off, dep_send.at[k, peer("depth", off)], dep_recv.at[k, off],
                 dep_s.at[k, off], dep_r.at[k, off])
            for off in range(1, Z)
        ])
    for copy in act_row:
        copy.wait_recv()
    for d in range(Z):
        act_out[d] = act_all[d].reshape(R * n_half, n_hid)
    for k in range(N_CHUNK):
        for copy in from_dep[k]:
            copy.wait_recv()
        total = dep_send[k, dep].astype(F32)
        for off in range(1, Z):
            total = total + dep_recv[k, off].astype(F32)
        in_out[:, k * chunk:(k + 1) * chunk] = total.astype(BF16)
    for copy in pending:
        copy.wait_send()


def grad_kernel(left_ref, right_ref, out_ref):
    out_ref[...] = over_tokens(left_ref[...], right_ref[...]).astype(BF16)


def shards(R, C, Z, tokens, cotangent, w_in, b_in, w_out):
    t, n_feat = tokens.shape
    n_hid = w_in.shape[1]
    n_d = w_out.shape[1]
    T = C * Z * t
    half = T // R
    chunk = n_feat // N_CHUNK
    cot = cotangent.reshape(t, Z, n_d).transpose(1, 0, 2)
    bias = lax.dynamic_slice_in_dim(b_in, lax.axis_index("depth") * n_hid, n_hid, 0).reshape(1, n_hid)
    vmem = pl.BlockSpec(memory_space=pltpu.VMEM)
    hbm = pl.BlockSpec(memory_space=pl.ANY)
    dma = pltpu.SemaphoreType.DMA
    shape = jax.ShapeDtypeStruct
    every_x, quarter_g, grad, act, b_grad, input_grad = pl.pallas_call(
        functools.partial(exchange_kernel, R, C, Z),
        out_shape=(
            shape((T, n_feat), BF16),
            shape((T, n_d), BF16),
            shape((T, n_hid), BF16),
            shape((Z, T, n_hid), BF16),
            shape((1, n_hid), F32),
            shape((t, n_feat), BF16),
        ),
        in_specs=[vmem, vmem, hbm, vmem, hbm],
        out_specs=(vmem,) * 6,
        scratch_shapes=[
            pltpu.VMEM(w_in.shape, BF16),
            pltpu.VMEM(w_out.shape, BF16),
            pltpu.VMEM((C * Z, t, n_feat), BF16),
            pltpu.VMEM((C * Z, t, n_d), BF16),
            pltpu.VMEM((R, half, n_hid), F32),
            pltpu.VMEM((R - 1, half, n_hid), F32),
            pltpu.VMEM((R, Z, half, n_hid), F32),
            pltpu.VMEM((R - 1, Z, half, n_hid), F32),
            pltpu.VMEM((Z, half, n_hid), BF16),
            pltpu.VMEM((Z, half, n_hid), BF16),
            pltpu.VMEM((Z, R, half, n_hid), BF16),
            pltpu.VMEM((R, half, n_hid), BF16),
            pltpu.VMEM((N_CHUNK, C, Z * t, chunk), BF16),
            pltpu.VMEM((N_CHUNK, C, Z * t, chunk), BF16),
            pltpu.VMEM((N_CHUNK, Z, t, chunk), BF16),
            pltpu.VMEM((N_CHUNK, Z, t, chunk), BF16),
            dma((2,)),
            dma((Z, C)), dma((Z, C)), dma((Z, C)), dma((Z, C)),
            dma((R - 1,)), dma((R - 1,)),
            dma((R - 1, Z)), dma((R - 1, Z)),
            dma((Z,)), dma((Z,)),
            dma((Z, R)), dma((Z, R)),
            dma((R,)), dma((R,)),
            dma((N_CHUNK, C)), dma((N_CHUNK, C)),
            dma((N_CHUNK, Z)), dma((N_CHUNK, Z)),
        ],
        compiler_params=pltpu.CompilerParams(
            collective_id=0, has_side_effects=True, vmem_limit_bytes=62 * 1024 * 1024
        ),
        cost_estimate=pl.CostEstimate(
            flops=6 * T * n_feat * n_hid, bytes_accessed=4 * n_feat * n_hid, transcendentals=half * n_hid
        ),
        name="exchange",
    )(tokens, cot, w_in, bias, w_out)

    block_f = block_of(n_feat)
    w_in_grad = pl.pallas_call(
        grad_kernel,
        grid=(n_feat // block_f,),
        in_specs=[
            pl.BlockSpec((T, block_f), lambda i: (0, i)),
            pl.BlockSpec((T, n_hid), lambda i: (0, 0)),
        ],
        out_specs=pl.BlockSpec((block_f, n_hid), lambda i: (i, 0)),
        out_shape=shape((n_feat, n_hid), BF16),
        name="w_in_grad",
    )(every_x, grad)
    block_h = block_of(n_hid)
    per = n_hid // block_h
    w_out_grad = pl.pallas_call(
        grad_kernel,
        grid=(Z, per),
        in_specs=[
            pl.BlockSpec((None, T, block_h), lambda d, j: (d, 0, j)),
            pl.BlockSpec((T, n_d), lambda d, j: (0, 0)),
        ],
        out_specs=pl.BlockSpec((block_h, n_d), lambda d, j: (d * per + j, 0)),
        out_shape=shape((Z * n_hid, n_d), BF16),
        name="w_out_grad",
    )(act, quarter_g)
    return (input_grad, w_in_grad, b_grad.reshape(n_hid), w_out_grad)


def solution(mesh):
    sizes = (mesh.shape["row"], mesh.shape["col"], mesh.shape["depth"])
    return jax.shard_map(
        functools.partial(shards, *sizes),
        mesh=mesh,
        in_specs=(
            P(("col", "depth"), "row"),
            P(("col", "depth"), "row"),
            P("row", ("col", "depth")),
            P("col"),
            P("col", ("row", "depth")),
        ),
        out_specs=(
            P(("col", "depth"), "row"),
            P("row", ("col", "depth")),
            P(("col", "depth")),
            P("col", ("row", "depth")),
        ),
        check_vma=False,
    )
```

time: 305 us -> 109 us (0.36)
  waiting for transfers between devices: 155 us -> 0 us
  Pallas kernels: 0 us -> 105 us
  matrix products: 59.8 us -> 0 us
  blocking collectives: 43.6 us -> 0 us
  local copies, waits for them, and re-layouts: 25.4 us -> 2.04 us
  between operations: 15.7 us -> 0.66 us
    reduce_scatter x4 -> x0, waiting for transfers between devices: 127 us -> none  [the longest x1 83.2 us: shards(): lax.psum_scatter(input_part, ('col', 'depth'), scatter_dimension=0, tiled...]
    pallas_call x0 -> x3, Pallas kernels: none -> 105 us  [the longest x1 78.8 us: shards(): pl.pallas_call(functools.partial(exchange_kernel, R, C, Z), out_shape=(sh...]
    dot_general x5 -> x0, matrix products: 59.8 us -> none  [the longest x2 29 us: against(): lax.dot_general(left, right, (((1,), (1,)), ((), ())), preferred_element_...]
    all_gather x3 -> x0, blocking collectives: 31.4 us -> none  [the longest x1 18.5 us: shards(): act_half = lax.all_gather(act, 'depth', axis=1, tiled=True)]
    all_gather x2 -> x0, waiting for transfers between devices: 26.6 us -> none  [the longest x1 26.6 us: shards(): every_x = lax.all_gather(tokens, ('col', 'depth'), axis=0, tiled=True)]
    unnamed x3 -> x5, local copies, waits for them, and re-layouts: 24.6 us -> 0.65 us
    all_to_all x1 -> x0, blocking collectives: 12.2 us -> none  [shards(): lax.all_to_all(cotangent, 'depth', split_axis=1, concat_axis=0, tiled=True)]
  transfers between devices with their start and end apart: 6 -> 0, of which waited for: 4 -> 0; matrix products, arithmetic and copies ran while one was open for 28% -> 0% of each run, Pallas kernels for 0% -> 0%
where the time goes in v2:
time: 109 us; the launch traced here: 108 us
  Pallas kernels  105 us (96%)
  local copies, waits for them, and re-layouts  2.04 us (2%)
    pallas_call x1, Pallas kernels, shards(): pl.pallas_call(functools.partial(exchange_kernel, R, C, Z), out_shape=(sh...  78.8 us
    pallas_call x1, Pallas kernels, shards(): pl.pallas_call(grad_kernel, grid=(Z, per), in_specs=[pl.BlockSpec((None,...  12.9 us
    pallas_call x1, Pallas kernels, shards(): pl.pallas_call(grad_kernel, grid=(n_feat // block_f,), in_specs=[pl.Block...  12.9 us

profile of v2, /device:TPU:0, one launch (start us, length us, event | category | flops | bytes accessed | tf_op | source)
XLA Modules:
  0.0 107.9 jit_solution(8963140295676313167)
XLA Ops:
  0.6 0.8 dynamic_slice.3
  1.4 0.6 reshape.18.b_ref
  2.0 78.8 %exchange.1 = (bf16[128,6144]{1,0:T(8,128)(2,1)}, bf16[128,1536]{1,0:T(8,128)(2,1)}, bf16[128,1536]{1,0:T(8,128)(2,1)}, bf16[4,128,1536]{2,1,0:T(8,128)(2,1)}, f...) custom-call(bf16[8,6144]{1,0:T(8,128)(2,1)} %tok_ref.1, bf16[4,8,1536]{2,1,0:T(8,128)(2,1)} %bitcast.3, ...), custom_call_target="tpu_custom_call" | custom-call | flops 7247757312 | bytes 37748736 | tf_op jit(solution)/shard_map/exchange/pallas_call | solution.py:278
  80.8 0.0 copy-start.1
  80.8 0.0 copy-start
  80.8 12.9 %w_out_grad.1 = bf16[6144,1536]{1,0:T(8,128)(2,1)} custom-call(bf16[4,128,1536]{2,1,0:T(8,128)(2,1)} %get-tuple-element.14.left_ref, bf16[128,1536]{1,0:T(8,128)(2,1)} %get-tuple-element.15.right_ref), custom_call_target="tpu_custom_call" | custom-call | tf_op jit(solution)/shard_map/w_out_grad/pallas_call | solution.py:340
  93.7 12.9 %w_in_grad.1 = bf16[6144,1536]{1,0:T(8,128)(2,1)} custom-call(bf16[128,6144]{1,0:T(8,128)(2,1)} %get-tuple-element.11.left_ref, bf16[128,1536]{1,0:T(8,128)(2,1)} %get-tuple-element.12.right_ref), custom_call_target="tpu_custom_call" | custom-call | tf_op jit(solution)/shard_map/w_in_grad/pallas_call | solution.py:327
  106.6 0.0 copy-done.1
  106.6 0.6 reduce
  107.3 0.0 copy-done
  107.3 0.6 copy.10
Async XLA Ops:
  80.8 25.9 %copy-start.1 = (f32[1,1536]{1,0:T(1,128)S(1)}, f32[1,1536]{1,0:T(1,128)}, u32[]{:S(2)}) copy-start(f32[1,1536]{1,0:T(1,128)} %get-tuple-element.13) | copy-start | bytes 18436
  80.8 26.5 %copy-start = (bf16[8,6144]{1,0:T(8,128)(2,1)S(1)}, bf16[8,6144]{1,0:T(8,128)(2,1)}, u32[]{:S(2)}) copy-start(bf16[8,6144]{1,0:T(8,128)(2,1)} %get-tuple-element.20) | copy-start | bytes 294916

commit v3 on v2

--- a/solution.py
+++ b/solution.py
@@ -11,7 +11,6 @@
 MESH = pl.DeviceIdType.MESH
 F32 = jnp.float32
 BF16 = jnp.bfloat16
-N_CHUNK = 4
 
 
 def gelu_pair(pre):
@@ -46,12 +45,15 @@
 def exchange_kernel(
     R, C, Z,
     tok_ref, cot_ref, w_in_hbm, b_ref, w_out_hbm,
-    x_out, g_out, grad_out, act_out, bias_out, in_out,
+    x_out, g_out, grad_out, act_out, bias_out, *rest,
+):
+    parts_out, rest = rest[:C], rest[C:]
+    (
     w_in_v, w_out_v, x_all, g_all, pre_part, pre_recv, back_part, back_recv,
-    back_send, back_depth, act_all, grad_all, col_send, col_recv, dep_send, dep_recv,
+    back_send, back_depth, act_all, grad_all, rolled,
     w_sem, x_s, x_r, g_s, g_r, pre_s, pre_r, br_s, br_r, bd_s, bd_r,
-    act_s, act_r, grad_s, grad_r, col_s, col_r, dep_s, dep_r,
-):
+    act_s, act_r, grad_s, grad_r,
+    ) = rest
     row, col, dep = lax.axis_index("row"), lax.axis_index("col"), lax.axis_index("depth")
     size = {"row": R, "col": C, "depth": Z}
     here = {"row": row, "col": col, "depth": dep}
@@ -130,32 +132,46 @@
     load_out.wait()
     n_half, n_hid = pre_part.shape[1], pre_part.shape[2]
     block_h = block_of(n_hid)
-    back_row = []
-    for d in range(Z):
-        def back_step(j, carry, d=d):
+    order = [*range(1, Z), 0]
+
+    def back_part_of(off):
+        d = peer("depth", off)
+
+        def back_step(j, carry):
             at = pl.ds(pl.multiple_of(d * n_hid + j * block_h, block_h), block_h)
             part = against(g_out[...], w_out_v[at, :])
-            back_part[:, d, :, cols_at(j, block_h)] = part.reshape(R, n_half, block_h)
+            back_part[:, off, :, cols_at(j, block_h)] = part.reshape(R, n_half, block_h)
             return carry
 
         lax.fori_loop(0, n_hid // block_h, back_step, 0)
-        for off in range(1, R):
-            back_row.append(send("row", off, back_part.at[peer("row", off), d], back_recv.at[off - 1, d],
-                                 br_s.at[off - 1, d], br_r.at[off - 1, d]))
-    for copy in back_row:
-        copy.wait_recv()
-
-    def back_sum(d):
-        total = back_part[row, d]
-        for off in range(1, R):
-            total = total + back_recv[off - 1, d]
+        return [
+            send("row", ro, back_part.at[peer("row", ro), off], back_recv.at[ro - 1, off],
+                 br_s.at[ro - 1, off], br_r.at[ro - 1, off])
+            for ro in range(1, R)
+        ]
+
+    def back_sum(off):
+        total = back_part[row, off]
+        for ro in range(1, R):
+            total = total + back_recv[ro - 1, off]
         return total
 
+    back_row = {}
     back_dep = []
-    for off in range(1, Z):
-        d = peer("depth", off)
-        back_send[off] = back_sum(d).astype(BF16)
-        back_dep.append(send("depth", off, back_send.at[off], back_depth.at[off], bd_s.at[off], bd_r.at[off]))
+
+    def back_on(off):
+        for copy in back_row[off]:
+            copy.wait_recv()
+        if off:
+            back_send[off] = back_sum(off).astype(BF16)
+            back_dep.append(send("depth", off, back_send.at[off], back_depth.at[off],
+                                 bd_s.at[off], bd_r.at[off]))
+
+    for n, off in enumerate(order):
+        back_row[off] = back_part_of(off)
+        if n:
+            back_on(order[n - 1])
+    back_on(order[-1])
 
     for copy in x_col:
         copy.wait_recv()
@@ -181,7 +197,7 @@
     pre = pre_part[row] + b_ref[...]
     for off in range(1, R):
         pre = pre + pre_recv[off - 1]
-    back = back_sum(dep)
+    back = back_sum(0)
     for off in range(1, Z):
         back = back + back_depth[off].astype(F32)
     act, slope = gelu_pair(pre)
@@ -205,23 +221,21 @@
         copy.wait_recv()
     grad_out[...] = grad_all[...].reshape(R * n_half, n_hid)
 
-    n_tok = dep_send.shape[2]
-    chunk = col_send.shape[3]
-    block_f = block_of(chunk)
-    from_col = []
-    for k in range(N_CHUNK):
-        def in_step(j, carry, k=k):
-            at = pl.ds(pl.multiple_of(k * chunk + j * block_f, block_f), block_f)
-            part = against(grad_out[...], w_in_v[at, :])
-            col_send[k, :, :, cols_at(j, block_f)] = part.astype(BF16).reshape(C, Z * n_tok, block_f)
-            return carry
-
-        lax.fori_loop(0, chunk // block_f, in_step, 0)
-        from_col.append([
-            send("col", off, col_send.at[k, peer("col", off)], col_recv.at[k, off],
-                 col_s.at[k, off], col_r.at[k, off])
-            for off in range(1, C)
-        ])
+    n_feat = x_out.shape[1]
+    n_tok = rolled.shape[0] // C
+    for off in range(C):
+        at = pl.ds(pl.multiple_of(peer("col", off) * n_tok, n_tok), n_tok)
+        rolled[off * n_tok:(off + 1) * n_tok, :] = grad_out[at, :]
+    block_f = block_of(n_feat)
+
+    def in_step(j, carry):
+        at = cols_at(j, block_f)
+        part = against(rolled[...], w_in_v[at, :])
+        for off in range(C):
+            parts_out[off][:, at] = part[off * n_tok:(off + 1) * n_tok, :].astype(parts_out[off].dtype)
+        return carry
+
+    lax.fori_loop(0, n_feat // block_f, in_step, 0)
     bias_out[...] = jnp.sum(grad_out[...].astype(F32), axis=0, keepdims=True)
     for off in range(1, Z):
         act_dep[off].wait_recv()
@@ -229,31 +243,10 @@
         for ro in range(1, R):
             act_row.append(send("row", ro, act_all.at[at, row], act_all.at[at, row],
                                 act_s.at[off, ro], act_r.at[off, ro]))
-    from_dep = []
-    for k in range(N_CHUNK):
-        for copy in from_col[k]:
-            copy.wait_recv()
-        total = col_send[k, col].astype(F32)
-        for off in range(1, C):
-            total = total + col_recv[k, off].astype(F32)
-        for d in range(Z):
-            dep_send[k, d] = total[d * n_tok:(d + 1) * n_tok, :].astype(BF16)
-        from_dep.append([
-            send("depth", off, dep_send.at[k, peer("depth", off)], dep_recv.at[k, off],
-                 dep_s.at[k, off], dep_r.at[k, off])
-            for off in range(1, Z)
-        ])
     for copy in act_row:
         copy.wait_recv()
     for d in range(Z):
         act_out[d] = act_all[d].reshape(R * n_half, n_hid)
-    for k in range(N_CHUNK):
-        for copy in from_dep[k]:
-            copy.wait_recv()
-        total = dep_send[k, dep].astype(F32)
-        for off in range(1, Z):
-            total = total + dep_recv[k, off].astype(F32)
-        in_out[:, k * chunk:(k + 1) * chunk] = total.astype(BF16)
     for copy in pending:
         copy.wait_send()
 
@@ -268,14 +261,13 @@
     n_d = w_out.shape[1]
     T = C * Z * t
     half = T // R
-    chunk = n_feat // N_CHUNK
     cot = cotangent.reshape(t, Z, n_d).transpose(1, 0, 2)
     bias = lax.dynamic_slice_in_dim(b_in, lax.axis_index("depth") * n_hid, n_hid, 0).reshape(1, n_hid)
     vmem = pl.BlockSpec(memory_space=pltpu.VMEM)
     hbm = pl.BlockSpec(memory_space=pl.ANY)
     dma = pltpu.SemaphoreType.DMA
     shape = jax.ShapeDtypeStruct
-    every_x, quarter_g, grad, act, b_grad, input_grad = pl.pallas_call(
+    every_x, quarter_g, grad, act, b_grad, *parts = pl.pallas_call(
         functools.partial(exchange_kernel, R, C, Z),
         out_shape=(
             shape((T, n_feat), BF16),
@@ -283,10 +275,10 @@
             shape((T, n_hid), BF16),
             shape((Z, T, n_hid), BF16),
             shape((1, n_hid), F32),
-            shape((t, n_feat), BF16),
-        ),
+            shape((Z * t, n_feat), F32),
+        ) + (shape((Z * t, n_feat), BF16),) * (C - 1),
         in_specs=[vmem, vmem, hbm, vmem, hbm],
-        out_specs=(vmem,) * 6,
+        out_specs=(vmem,) * (5 + C),
         scratch_shapes=[
             pltpu.VMEM(w_in.shape, BF16),
             pltpu.VMEM(w_out.shape, BF16),
@@ -300,10 +292,7 @@
             pltpu.VMEM((Z, half, n_hid), BF16),
             pltpu.VMEM((Z, R, half, n_hid), BF16),
             pltpu.VMEM((R, half, n_hid), BF16),
-            pltpu.VMEM((N_CHUNK, C, Z * t, chunk), BF16),
-            pltpu.VMEM((N_CHUNK, C, Z * t, chunk), BF16),
-            pltpu.VMEM((N_CHUNK, Z, t, chunk), BF16),
-            pltpu.VMEM((N_CHUNK, Z, t, chunk), BF16),
+            pltpu.VMEM((T, n_hid), BF16),
             dma((2,)),
             dma((Z, C)), dma((Z, C)), dma((Z, C)), dma((Z, C)),
             dma((R - 1,)), dma((R - 1,)),
@@ -311,8 +300,6 @@
             dma((Z,)), dma((Z,)),
             dma((Z, R)), dma((Z, R)),
             dma((R,)), dma((R,)),
-            dma((N_CHUNK, C)), dma((N_CHUNK, C)),
-            dma((N_CHUNK, Z)), dma((N_CHUNK, Z)),
         ],
         compiler_params=pltpu.CompilerParams(
             collective_id=0, has_side_effects=True, vmem_limit_bytes=62 * 1024 * 1024
@@ -323,6 +310,13 @@
         name="exchange",
     )(tokens, cot, w_in, bias, w_out)
 
+    def shifted(value, axis, n, off):
+        return lax.ppermute(value, axis, [(i, (i + off) % n) for i in range(n)])
+
+    from_col = [shifted(parts[off], "col", C, off) for off in range(1, C)]
+    cost = pl.CostEstimate(
+        flops=2 * T * n_feat * n_hid, bytes_accessed=2 * n_feat * n_hid, transcendentals=0
+    )
     block_f = block_of(n_feat)
     w_in_grad = pl.pallas_call(
         grad_kernel,
@@ -333,8 +327,20 @@
         ],
         out_specs=pl.BlockSpec((block_f, n_hid), lambda i: (i, 0)),
         out_shape=shape((n_feat, n_hid), BF16),
+        cost_estimate=cost,
         name="w_in_grad",
     )(every_x, grad)
+    total = parts[0]
+    for value in from_col:
+        total = total + value.astype(F32)
+    act, total, w_in_grad = lax.optimization_barrier((act, total, w_in_grad))
+    total = total.reshape(Z, t, n_feat)
+
+    def for_depth(off):
+        at = lax.rem(lax.axis_index("depth") + off, Z)
+        return lax.dynamic_index_in_dim(total, at, 0, keepdims=False)
+
+    from_dep = [shifted(for_depth(off).astype(BF16), "depth", Z, off) for off in range(1, Z)]
     block_h = block_of(n_hid)
     per = n_hid // block_h
     w_out_grad = pl.pallas_call(
@@ -346,8 +352,13 @@
         ],
         out_specs=pl.BlockSpec((block_h, n_d), lambda d, j: (d * per + j, 0)),
         out_shape=shape((Z * n_hid, n_d), BF16),
+        cost_estimate=cost,
         name="w_out_grad",
     )(act, quarter_g)
+    input_sum = for_depth(0)
+    for value in from_dep:
+        input_sum = input_sum + value.astype(F32)
+    input_grad = input_sum.astype(BF16)
     return (input_grad, w_in_grad, b_grad.reshape(n_hid), w_out_grad)
 
 

time: 109 us -> 106 us (0.972)
  Pallas kernels: 105 us -> 85 us
  starting transfers between devices: 0 us -> 13 us
  waiting for transfers between devices: 0 us -> 2.78 us
  other arithmetic: 0.62 us -> 2.16 us
    pallas_call x1, Pallas kernels: 78.8 us -> 59.2 us  [shards(): pl.pallas_call(functools.partial(exchange_kernel, R, C, Z), out_shape=(sh...]
    ppermute x0 -> x6, starting transfers between devices: none -> 13 us  [shifted(): return lax.ppermute(value, axis, [(i, (i + off) % n) for i in range(n)])]
    ppermute x0 -> x6, waiting for transfers between devices: none -> 2.78 us  [shifted(): return lax.ppermute(value, axis, [(i, (i + off) % n) for i in range(n)])]
  transfers between devices with their start and end apart: 0 -> 6, of which waited for: 0 -> 1; matrix products, arithmetic and copies ran while one was open for 0% -> 1% of each run, Pallas kernels for 0% -> 25%
where the time goes in v3:
time: 106 us; the launch traced here: 105 us
  Pallas kernels  85 us (80%)
  starting transfers between devices  13 us (12%)
  waiting for transfers between devices  2.78 us (3%)
  other arithmetic  2.16 us (2%)
  local copies, waits for them, and re-layouts  1.43 us (1%)
    pallas_call x1, Pallas kernels, shards(): pl.pallas_call(functools.partial(exchange_kernel, R, C, Z), out_shape=(sh...  59.2 us
    ppermute x6, starting transfers between devices, shifted(): return lax.ppermute(value, axis, [(i, (i + off) % n) for i in range(n)])  13 us
    pallas_call x1, Pallas kernels, shards(): pl.pallas_call(grad_kernel, grid=(n_feat // block_f,), in_specs=[pl.Block...  12.9 us
    pallas_call x1, Pallas kernels, shards(): pl.pallas_call(grad_kernel, grid=(Z, per), in_specs=[pl.BlockSpec((None,...  12.9 us
    ppermute x6, waiting for transfers between devices, shifted(): return lax.ppermute(value, axis, [(i, (i + off) % n) for i in range(n)])  2.78 us
  transfers between devices with their start and end apart: 6, of which 1 were waited for; matrix products, arithmetic and copies ran while one was open for 1% of the time, Pallas kernels for 25%

profile of v3, /device:TPU:0, one launch (start us, length us, event | category | flops | bytes accessed | tf_op | source)
XLA Modules:
  0.0 105.1 jit_solution(5978247578926753726)
XLA Ops:
  0.6 0.8 dynamic_slice.16
  1.4 0.6 reshape.24.b_ref
  2.0 59.2 %exchange.1 = (bf16[128,6144]{1,0:T(8,128)(2,1)}, bf16[128,1536]{1,0:T(8,128)(2,1)}, bf16[128,1536]{1,0:T(8,128)(2,1)}, bf16[4,128,1536]{2,1,0:T(8,128)(2,1)}, f...) custom-call(bf16[8,6144]{1,0:T(8,128)(2,1)} %tok_ref.1, ...), custom_call_target="tpu_custom_call" | custom-call | flops 7247757312 | bytes 37748736 | tf_op jit(solution)/shard_map/exchange/pallas_call | solution.py:270
  61.2 0.0 copy-start
  61.2 1.2 %collective-permute-start = (bf16[32,6144]{1,0:T(8,128)(2,1)}, bf16[32,6144]{1,0:T(8,128)(2,1)S(1)}, u32[]{:S(2)}, u32[]{:S(2)}) collective-permute-start(bf16[32,6144]{1,0:T(8,128)(2,1)} %get-tuple-element.18), channel_id=1, source_target_pairs={{0,4},{4,8},{8,12},{12,0},{1,5},{5,9},{9,13},{13,1},{2,6},{6,10},{... | collective-permute-start | bytes 1179656 | tf_op jit(solution)/shard_map/ppermute | solution.py:314
  62.4 1.5 %collective-permute-start.1 = (bf16[32,6144]{1,0:T(8,128)(2,1)}, bf16[32,6144]{1,0:T(8,128)(2,1)S(1)}, u32[]{:S(2)}, u32[]{:S(2)}) collective-permute-start(bf16[32,6144]{1,0:T(8,128)(2,1)} %get-tuple-element.19), channel_id=1, source_target_pairs={{0,8},{4,12},{8,0},{12,4},{1,9},{5,13},{9,1},{13,5},{2,10},{6,14},... | collective-permute-start | bytes 1179656 | tf_op jit(solution)/shard_map/ppermute | solution.py:314
  63.9 1.5 %collective-permute-start.2 = (bf16[32,6144]{1,0:T(8,128)(2,1)}, bf16[32,6144]{1,0:T(8,128)(2,1)S(1)}, u32[]{:S(2)}, u32[]{:S(2)}) collective-permute-start(bf16[32,6144]{1,0:T(8,128)(2,1)} %get-tuple-element.20), channel_id=1, source_target_pairs={{0,12},{4,0},{8,4},{12,8},{1,13},{5,1},{9,5},{13,9},{2,14},{6,2},{... | collective-permute-start | bytes 1179656 | tf_op jit(solution)/shard_map/ppermute | solution.py:314
  65.4 1.3 %reduce = f32[1536]{0:T(1024)} reduce(f32[1,1536]{1,0:T(1,128)} %get-tuple-element.25, f32[]{:T(128)} %constant.38), dimensions={0}, to_apply=%get-tuple-element.25.reduce_sub_computation | reduce | bytes 12292 | tf_op jit(solution)/shard_map/exchange/pallas_call | solution.py:270
  66.7 12.9 %w_in_grad.1 = bf16[6144,1536]{1,0:T(8,128)(2,1)} custom-call(bf16[128,6144]{1,0:T(8,128)(2,1)} %get-tuple-element.21.left_ref, bf16[128,1536]{1,0:T(8,128)(2,1)} %get-tuple-element.22.right_ref), custom_call_target="tpu_custom_call" | custom-call | flops 2415919104 | bytes 18874368 | tf_op jit(solution)/shard_map/w_in_grad/pallas_call | solution.py:321
  79.6 0.0 collective-permute-done
  79.6 2.8 %collective-permute-done.1 = bf16[32,6144]{1,0:T(8,128)(2,1)S(1)} collective-permute-done((bf16[32,6144]{1,0:T(8,128)(2,1)}, bf16[32,6144]{1,0:T(8,128)(2,1)S(1)}, u32[]{:S(2)}, u32[]{:S(2)}) %collective-permute-start.1) | collective-permute-done | bytes 393248 | tf_op jit(solution)/shard_map/ppermute | solution.py:314
  82.3 0.0 collective-permute-done.2
  82.3 0.0 copy-done
  82.3 0.2 convert_add_fusion
  82.6 4.5 %collective-permute-start.3 = (bf16[8,6144]{1,0:T(8,128)(2,1)S(1)}, bf16[8,6144]{1,0:T(8,128)(2,1)S(1)}, u32[]{:S(2)}, u32[]{:S(2)}) collective-permute-start(bf16[8,6144]{1,0:T(8,128)(2,1)S(1)} %get-tuple-element.28), channel_id=1, source_target_pairs={{0,1},{1,2},{2,3},{3,0},{4,5},{5,6},{6,7},{7,4},{8,9},{9,10},{10,1... | collective-permute-start | bytes 294920 | tf_op jit(solution)/shard_map/ppermute | solution.py:314
  87.0 4.0 %collective-permute-start.5 = (bf16[8,6144]{1,0:T(8,128)(2,1)S(1)}, bf16[8,6144]{1,0:T(8,128)(2,1)S(1)}, u32[]{:S(2)}, u32[]{:S(2)}) collective-permute-start(bf16[8,6144]{1,0:T(8,128)(2,1)S(1)} %get-tuple-element.29), channel_id=1, source_target_pairs={{0,3},{1,0},{2,1},{3,2},{4,7},{5,4},{6,5},{7,6},{8,11},{9,8},{10,9... | collective-permute-start | bytes 294920 | tf_op jit(solution)/shard_map/ppermute | solution.py:314
  91.0 0.5 collective-permute-start.4
  91.5 12.9 %w_out_grad.1 = bf16[6144,1536]{1,0:T(8,128)(2,1)} custom-call(bf16[4,128,1536]{2,1,0:T(8,128)(2,1)} %get-tuple-element.26.left_ref, bf16[128,1536]{1,0:T(8,128)(2,1)} %get-tuple-element.27.right_ref), custom_call_target="tpu_custom_call" | custom-call | flops 2415919104 | bytes 18874368 | tf_op jit(solution)/shard_map/w_out_grad/pallas_call | solution.py:346
  104.4 0.0 collective-permute-done.3
  104.4 0.0 collective-permute-done.5
  104.4 0.0 collective-permute-done.4
  104.4 0.7 fusion.2
  (1 shorter events, 0.0 us)
Async XLA Ops:
  61.2 21.1 %copy-start = (f32[32,6144]{1,0:T(8,128)S(1)}, f32[32,6144]{1,0:T(8,128)}, u32[]{:S(2)}) copy-start(f32[32,6144]{1,0:T(8,128)} %get-tuple-element.17) | copy-start | bytes 2359300
  61.2 18.3 %collective-permute-start = (bf16[32,6144]{1,0:T(8,128)(2,1)}, bf16[32,6144]{1,0:T(8,128)(2,1)S(1)}, u32[]{:S(2)}, u32[]{:S(2)}) collective-permute-start(bf16[32,6144]{1,0:T(8,128)(2,1)} %get-tuple-element.18), channel_id=1, source_target_pairs={{0,4},{4,8},{8,12},{12,0},{1,5},{5,9},{9,13},{13,1},{2,6},{6,10},{... | collective-permute-start | bytes 1179656 | tf_op jit(solution)/shard_map/ppermute | solution.py:314
  62.4 19.9 %collective-permute-start.1 = (bf16[32,6144]{1,0:T(8,128)(2,1)}, bf16[32,6144]{1,0:T(8,128)(2,1)S(1)}, u32[]{:S(2)}, u32[]{:S(2)}) collective-permute-start(bf16[32,6144]{1,0:T(8,128)(2,1)} %get-tuple-element.19), channel_id=1, source_target_pairs={{0,8},{4,12},{8,0},{12,4},{1,9},{5,13},{9,1},{13,5},{2,10},{6,14},... | collective-permute-start | bytes 1179656 | tf_op jit(solution)/shard_map/ppermute | solution.py:314
  63.9 18.4 %collective-permute-start.2 = (bf16[32,6144]{1,0:T(8,128)(2,1)}, bf16[32,6144]{1,0:T(8,128)(2,1)S(1)}, u32[]{:S(2)}, u32[]{:S(2)}) collective-permute-start(bf16[32,6144]{1,0:T(8,128)(2,1)} %get-tuple-element.20), channel_id=1, source_target_pairs={{0,12},{4,0},{8,4},{12,8},{1,13},{5,1},{9,5},{13,9},{2,14},{6,2},{... | collective-permute-start | bytes 1179656 | tf_op jit(solution)/shard_map/ppermute | solution.py:314
  82.6 21.8 %collective-permute-start.3 = (bf16[8,6144]{1,0:T(8,128)(2,1)S(1)}, bf16[8,6144]{1,0:T(8,128)(2,1)S(1)}, u32[]{:S(2)}, u32[]{:S(2)}) collective-permute-start(bf16[8,6144]{1,0:T(8,128)(2,1)S(1)} %get-tuple-element.28), channel_id=1, source_target_pairs={{0,1},{1,2},{2,3},{3,0},{4,5},{5,6},{6,7},{7,4},{8,9},{9,10},{10,1... | collective-permute-start | bytes 294920 | tf_op jit(solution)/shard_map/ppermute | solution.py:314
  87.0 17.4 %collective-permute-start.5 = (bf16[8,6144]{1,0:T(8,128)(2,1)S(1)}, bf16[8,6144]{1,0:T(8,128)(2,1)S(1)}, u32[]{:S(2)}, u32[]{:S(2)}) collective-permute-start(bf16[8,6144]{1,0:T(8,128)(2,1)S(1)} %get-tuple-element.29), channel_id=1, source_target_pairs={{0,3},{1,0},{2,1},{3,2},{4,7},{5,4},{6,5},{7,6},{8,11},{9,8},{10,9... | collective-permute-start | bytes 294920 | tf_op jit(solution)/shard_map/ppermute | solution.py:314
  91.0 13.4 %collective-permute-start.4 = (bf16[8,6144]{1,0:T(8,128)(2,1)S(1)}, bf16[8,6144]{1,0:T(8,128)(2,1)S(1)}, u32[]{:S(2)}, u32[]{:S(2)}) collective-permute-start(bf16[8,6144]{1,0:T(8,128)(2,1)S(1)} %get-tuple-element.30), channel_id=1, source_target_pairs={{0,2},{1,3},{2,0},{3,1},{4,6},{5,7},{6,4},{7,5},{8,10},{9,11},{10,... | collective-permute-start | bytes 294920 | tf_op jit(solution)/shard_map/ppermute | solution.py:314

commit v4 on v3

--- a/solution.py
+++ b/solution.py
@@ -251,8 +251,15 @@
         copy.wait_send()
 
 
-def grad_kernel(left_ref, right_ref, out_ref):
-    out_ref[...] = over_tokens(left_ref[...], right_ref[...]).astype(BF16)
+def grad_kernel(left_ref, right_ref, *refs):
+    out_ref = refs[-1]
+    rows, cols = out_ref.shape
+    tall, wide = block_of(rows, 256), block_of(cols, 256)
+    for m in range(0, rows, tall):
+        left = left_ref[:, m:m + tall].T
+        for n in range(0, cols, wide):
+            part = jnp.dot(left, right_ref[:, n:n + wide], preferred_element_type=F32)
+            out_ref[m:m + tall, n:n + wide] = part.astype(BF16)
 
 
 def shards(R, C, Z, tokens, cotangent, w_in, b_in, w_out):
@@ -315,7 +322,7 @@
 
     from_col = [shifted(parts[off], "col", C, off) for off in range(1, C)]
     cost = pl.CostEstimate(
-        flops=2 * T * n_feat * n_hid, bytes_accessed=2 * n_feat * n_hid, transcendentals=0
+        flops=T * n_feat * n_hid, bytes_accessed=n_feat * n_hid, transcendentals=0
     )
     block_f = block_of(n_feat)
     w_in_grad = pl.pallas_call(
@@ -330,10 +337,31 @@
         cost_estimate=cost,
         name="w_in_grad",
     )(every_x, grad)
+    block_h = block_of(n_hid)
+    per = n_hid // block_h
+    w_out_shape = shape((Z * n_hid, n_d), BF16)
+
+    def w_out_part(first, last, *held):
+        return pl.pallas_call(
+            grad_kernel,
+            grid=(last - first, per),
+            in_specs=[
+                pl.BlockSpec((None, T, block_h), lambda d, j: (first + d, 0, j)),
+                pl.BlockSpec((T, n_d), lambda d, j: (0, 0)),
+            ] + [hbm] * len(held),
+            out_specs=pl.BlockSpec((block_h, n_d), lambda d, j: ((first + d) * per + j, 0)),
+            out_shape=w_out_shape,
+            input_output_aliases={2: 0} if held else {},
+            cost_estimate=cost,
+            name="w_out_grad",
+        )(act, quarter_g, *held)
+
+    w_out_grad = w_out_part(0, Z // 2)
+    *from_col, w_in_grad, w_out_grad = lax.optimization_barrier((*from_col, w_in_grad, w_out_grad))
     total = parts[0]
     for value in from_col:
         total = total + value.astype(F32)
-    act, total, w_in_grad = lax.optimization_barrier((act, total, w_in_grad))
+    total, w_out_grad = lax.optimization_barrier((total, w_out_grad))
     total = total.reshape(Z, t, n_feat)
 
     def for_depth(off):
@@ -341,20 +369,7 @@
         return lax.dynamic_index_in_dim(total, at, 0, keepdims=False)
 
     from_dep = [shifted(for_depth(off).astype(BF16), "depth", Z, off) for off in range(1, Z)]
-    block_h = block_of(n_hid)
-    per = n_hid // block_h
-    w_out_grad = pl.pallas_call(
-        grad_kernel,
-        grid=(Z, per),
-        in_specs=[
-            pl.BlockSpec((None, T, block_h), lambda d, j: (d, 0, j)),
-            pl.BlockSpec((T, n_d), lambda d, j: (0, 0)),
-        ],
-        out_specs=pl.BlockSpec((block_h, n_d), lambda d, j: (d * per + j, 0)),
-        out_shape=shape((Z * n_hid, n_d), BF16),
-        cost_estimate=cost,
-        name="w_out_grad",
-    )(act, quarter_g)
+    w_out_grad = w_out_part(Z // 2, Z, w_out_grad)
     input_sum = for_depth(0)
     for value in from_dep:
         input_sum = input_sum + value.astype(F32)

time: 106 us -> 106 us (level)
  Pallas kernels: 85 us -> 86.8 us
  waiting for transfers between devices: 2.78 us -> 1.11 us
    pallas_call x1 -> x2, Pallas kernels: 12.9 us -> 14.6 us  [w_out_part(): pl.pallas_call(grad_kernel, grid=(last - first, per), in_specs=[pl.BlockS...]
    ppermute x6, waiting for transfers between devices: 2.78 us -> 1.11 us  [shifted(): return lax.ppermute(value, axis, [(i, (i + off) % n) for i in range(n)])]
  transfers between devices with their start and end apart: 6 -> 6, of which waited for: 1 -> 1; matrix products, arithmetic and copies ran while one was open for 1% -> 1% of each run, Pallas kernels for 25% -> 26%
where the time goes in v4:
time: 106 us; the launch traced here: 105 us
  Pallas kernels  86.8 us (82%)
  starting transfers between devices  13 us (12%)
  other arithmetic  2.15 us (2%)
  local copies, waits for them, and re-layouts  1.43 us (1%)
  waiting for transfers between devices  1.11 us (1%)
    pallas_call x1, Pallas kernels, shards(): pl.pallas_call(functools.partial(exchange_kernel, R, C, Z), out_shape=(sh...  59.2 us
    pallas_call x2, Pallas kernels, w_out_part(): pl.pallas_call(grad_kernel, grid=(last - first, per), in_specs=[pl.BlockS...  14.6 us
    ppermute x6, starting transfers between devices, shifted(): return lax.ppermute(value, axis, [(i, (i + off) % n) for i in range(n)])  13 us
    pallas_call x1, Pallas kernels, shards(): pl.pallas_call(grad_kernel, grid=(n_feat // block_f,), in_specs=[pl.Block...  13 us
  transfers between devices with their start and end apart: 6, of which 1 were waited for; matrix products, arithmetic and copies ran while one was open for 1% of the time, Pallas kernels for 26%

profile of v4, /device:TPU:0, one launch (start us, length us, event | category | flops | bytes accessed | tf_op | source)
XLA Modules:
  0.0 105.2 jit_solution(5330143004407923372)
XLA Ops:
  0.6 0.8 dynamic_slice.16
  1.4 0.6 reshape.24.b_ref
  2.0 59.2 %exchange.1 = (bf16[128,6144]{1,0:T(8,128)(2,1)}, bf16[128,1536]{1,0:T(8,128)(2,1)}, bf16[128,1536]{1,0:T(8,128)(2,1)}, bf16[4,128,1536]{2,1,0:T(8,128)(2,1)}, f...) custom-call(bf16[8,6144]{1,0:T(8,128)(2,1)} %tok_ref.1, ...), custom_call_target="tpu_custom_call" | custom-call | flops 7247757312 | bytes 37748736 | tf_op jit(solution)/shard_map/exchange/pallas_call | solution.py:277
  61.2 1.2 %collective-permute-start = (bf16[32,6144]{1,0:T(8,128)(2,1)}, bf16[32,6144]{1,0:T(8,128)(2,1)S(1)}, u32[]{:S(2)}, u32[]{:S(2)}) collective-permute-start(bf16[32,6144]{1,0:T(8,128)(2,1)} %get-tuple-element.21), channel_id=1, source_target_pairs={{0,4},{4,8},{8,12},{12,0},{1,5},{5,9},{9,13},{13,1},{2,6},{6,10},{... | collective-permute-start | bytes 1179656 | tf_op jit(solution)/shard_map/ppermute | solution.py:321
  62.4 1.5 %collective-permute-start.1 = (bf16[32,6144]{1,0:T(8,128)(2,1)}, bf16[32,6144]{1,0:T(8,128)(2,1)S(1)}, u32[]{:S(2)}, u32[]{:S(2)}) collective-permute-start(bf16[32,6144]{1,0:T(8,128)(2,1)} %get-tuple-element.22), channel_id=1, source_target_pairs={{0,8},{4,12},{8,0},{12,4},{1,9},{5,13},{9,1},{13,5},{2,10},{6,14},... | collective-permute-start | bytes 1179656 | tf_op jit(solution)/shard_map/ppermute | solution.py:321
  63.9 1.5 %collective-permute-start.2 = (bf16[32,6144]{1,0:T(8,128)(2,1)}, bf16[32,6144]{1,0:T(8,128)(2,1)S(1)}, u32[]{:S(2)}, u32[]{:S(2)}) collective-permute-start(bf16[32,6144]{1,0:T(8,128)(2,1)} %get-tuple-element.23), channel_id=1, source_target_pairs={{0,12},{4,0},{8,4},{12,8},{1,13},{5,1},{9,5},{13,9},{2,14},{6,2},{... | collective-permute-start | bytes 1179656 | tf_op jit(solution)/shard_map/ppermute | solution.py:321
  65.4 1.3 %reduce = f32[1536]{0:T(1024)} reduce(f32[1,1536]{1,0:T(1,128)} %get-tuple-element.34, f32[]{:T(128)} %constant.38), dimensions={0}, to_apply=%get-tuple-element.34.reduce_sub_computation | reduce | bytes 12292 | tf_op jit(solution)/shard_map/exchange/pallas_call | solution.py:277
  66.7 0.0 copy-start
  66.7 13.0 %w_in_grad.1 = bf16[6144,1536]{1,0:T(8,128)(2,1)} custom-call(bf16[128,6144]{1,0:T(8,128)(2,1)} %get-tuple-element.24.left_ref, bf16[128,1536]{1,0:T(8,128)(2,1)} %get-tuple-element.25.right_ref), custom_call_target="tpu_custom_call" | custom-call | flops 1207959552 | bytes 9437184 | tf_op jit(solution)/shard_map/w_in_grad/pallas_call | solution.py:328
  79.6 7.3 %w_out_grad.2.refs_0_ = bf16[6144,1536]{1,0:T(8,128)(2,1)} custom-call(bf16[4,128,1536]{2,1,0:T(8,128)(2,1)} %get-tuple-element.26.left_ref, bf16[128,1536]{1,0:T(8,128)(2,1)} %get-tuple-element.27.right_ref), custom_call_target="tpu_custom_call" | custom-call | flops 1207959552 | bytes 9437184 | tf_op jit(solution)/shard_map/w_out_grad/pallas_call | solution.py:345
  86.9 0.0 collective-permute-done
  86.9 0.0 collective-permute-done.1
  87.0 0.0 collective-permute-done.2
  87.0 0.0 copy-done
  87.0 0.2 convert_add_fusion
  87.2 4.5 %collective-permute-start.3 = (bf16[8,6144]{1,0:T(8,128)(2,1)S(1)}, bf16[8,6144]{1,0:T(8,128)(2,1)S(1)}, u32[]{:S(2)}, u32[]{:S(2)}) collective-permute-start(bf16[8,6144]{1,0:T(8,128)(2,1)S(1)} %get-tuple-element.36), channel_id=1, source_target_pairs={{0,1},{1,2},{2,3},{3,0},{4,5},{5,6},{6,7},{7,4},{8,9},{9,10},{10,1... | collective-permute-start | bytes 294920 | tf_op jit(solution)/shard_map/ppermute | solution.py:321
  91.7 3.9 %collective-permute-start.5 = (bf16[8,6144]{1,0:T(8,128)(2,1)S(1)}, bf16[8,6144]{1,0:T(8,128)(2,1)S(1)}, u32[]{:S(2)}, u32[]{:S(2)}) collective-permute-start(bf16[8,6144]{1,0:T(8,128)(2,1)S(1)} %get-tuple-element.37), channel_id=1, source_target_pairs={{0,3},{1,0},{2,1},{3,2},{4,7},{5,4},{6,5},{7,6},{8,11},{9,8},{10,9... | collective-permute-start | bytes 294920 | tf_op jit(solution)/shard_map/ppermute | solution.py:321
  95.6 0.5 collective-permute-start.4
  96.1 7.3 %w_out_grad.3 = bf16[6144,1536]{1,0:T(8,128)(2,1)} custom-call(bf16[4,128,1536]{2,1,0:T(8,128)(2,1)} %get-tuple-element.26.left_ref, bf16[128,1536]{1,0:T(8,128)(2,1)} %get-tuple-element.27.right_ref, bf16[6144,1536]{1,0:T(8,128)(2,1)} %w_out_grad.2.refs_0_), custom_call_target="tpu_custom_call", output_to_operand_aliasing={{}: (2, {})} | custom-call | flops 1207959552 | bytes 9437184 | tf_op jit(solution)/shard_map/w_out_grad/pallas_call | solution.py:345
  103.4 0.0 collective-permute-done.3
  103.4 0.0 collective-permute-done.5
  103.4 1.1 %collective-permute-done.4 = bf16[8,6144]{1,0:T(8,128)(2,1)S(1)} collective-permute-done((bf16[8,6144]{1,0:T(8,128)(2,1)S(1)}, bf16[8,6144]{1,0:T(8,128)(2,1)S(1)}, u32[]{:S(2)}, u32[]{:S(2)}) %collective-permute-start.4) | collective-permute-done | bytes 98336 | tf_op jit(solution)/shard_map/ppermute | solution.py:321
  104.5 0.7 fusion.2
  (1 shorter events, 0.0 us)
Async XLA Ops:
  61.2 25.7 %collective-permute-start = (bf16[32,6144]{1,0:T(8,128)(2,1)}, bf16[32,6144]{1,0:T(8,128)(2,1)S(1)}, u32[]{:S(2)}, u32[]{:S(2)}) collective-permute-start(bf16[32,6144]{1,0:T(8,128)(2,1)} %get-tuple-element.21), channel_id=1, source_target_pairs={{0,4},{4,8},{8,12},{12,0},{1,5},{5,9},{9,13},{13,1},{2,6},{6,10},{... | collective-permute-start | bytes 1179656 | tf_op jit(solution)/shard_map/ppermute | solution.py:321
  62.4 24.5 %collective-permute-start.1 = (bf16[32,6144]{1,0:T(8,128)(2,1)}, bf16[32,6144]{1,0:T(8,128)(2,1)S(1)}, u32[]{:S(2)}, u32[]{:S(2)}) collective-permute-start(bf16[32,6144]{1,0:T(8,128)(2,1)} %get-tuple-element.22), channel_id=1, source_target_pairs={{0,8},{4,12},{8,0},{12,4},{1,9},{5,13},{9,1},{13,5},{2,10},{6,14},... | collective-permute-start | bytes 1179656 | tf_op jit(solution)/shard_map/ppermute | solution.py:321
  63.9 23.1 %collective-permute-start.2 = (bf16[32,6144]{1,0:T(8,128)(2,1)}, bf16[32,6144]{1,0:T(8,128)(2,1)S(1)}, u32[]{:S(2)}, u32[]{:S(2)}) collective-permute-start(bf16[32,6144]{1,0:T(8,128)(2,1)} %get-tuple-element.23), channel_id=1, source_target_pairs={{0,12},{4,0},{8,4},{12,8},{1,13},{5,1},{9,5},{13,9},{2,14},{6,2},{... | collective-permute-start | bytes 1179656 | tf_op jit(solution)/shard_map/ppermute | solution.py:321
  66.7 20.3 %copy-start = (f32[32,6144]{1,0:T(8,128)S(1)}, f32[32,6144]{1,0:T(8,128)}, u32[]{:S(2)}) copy-start(f32[32,6144]{1,0:T(8,128)} %get-tuple-element.20) | copy-start | bytes 2359300
  87.2 16.2 %collective-permute-start.3 = (bf16[8,6144]{1,0:T(8,128)(2,1)S(1)}, bf16[8,6144]{1,0:T(8,128)(2,1)S(1)}, u32[]{:S(2)}, u32[]{:S(2)}) collective-permute-start(bf16[8,6144]{1,0:T(8,128)(2,1)S(1)} %get-tuple-element.36), channel_id=1, source_target_pairs={{0,1},{1,2},{2,3},{3,0},{4,5},{5,6},{6,7},{7,4},{8,9},{9,10},{10,1... | collective-permute-start | bytes 294920 | tf_op jit(solution)/shard_map/ppermute | solution.py:321
  91.7 11.7 %collective-permute-start.5 = (bf16[8,6144]{1,0:T(8,128)(2,1)S(1)}, bf16[8,6144]{1,0:T(8,128)(2,1)S(1)}, u32[]{:S(2)}, u32[]{:S(2)}) collective-permute-start(bf16[8,6144]{1,0:T(8,128)(2,1)S(1)} %get-tuple-element.37), channel_id=1, source_target_pairs={{0,3},{1,0},{2,1},{3,2},{4,7},{5,4},{6,5},{7,6},{8,11},{9,8},{10,9... | collective-permute-start | bytes 294920 | tf_op jit(solution)/shard_map/ppermute | solution.py:321
  95.6 8.9 %collective-permute-start.4 = (bf16[8,6144]{1,0:T(8,128)(2,1)S(1)}, bf16[8,6144]{1,0:T(8,128)(2,1)S(1)}, u32[]{:S(2)}, u32[]{:S(2)}) collective-permute-start(bf16[8,6144]{1,0:T(8,128)(2,1)S(1)} %get-tuple-element.38), channel_id=1, source_target_pairs={{0,2},{1,3},{2,0},{3,1},{4,6},{5,7},{6,4},{7,5},{8,10},{9,11},{10,... | collective-permute-start | bytes 294920 | tf_op jit(solution)/shard_map/ppermute | solution.py:321

commit v5 on v3

--- a/solution.py
+++ b/solution.py
@@ -251,8 +251,39 @@
         copy.wait_send()
 
 
-def grad_kernel(left_ref, right_ref, out_ref):
-    out_ref[...] = over_tokens(left_ref[...], right_ref[...]).astype(BF16)
+def grad_kernel(first, n_parts, left_ref, right_ref, *refs):
+    out_ref, held, sems = refs[-3:]
+    n_left, cols = left_ref.shape[-1], right_ref.shape[-1]
+    block = block_of(n_left)
+    per = n_left // block
+    tall, wide = block_of(block, 256), block_of(cols, 256)
+
+    def copy_of(i):
+        start = pl.multiple_of(i * block, block)
+        return pltpu.make_async_copy(
+            held.at[pl.ds(start, block), :],
+            out_ref.at[pl.ds(pl.multiple_of(first * n_left + start, block), block), :],
+            sems.at[i],
+        )
+
+    def make(i, carry):
+        d, j = i // per, lax.rem(i, per)
+        for m in range(0, block, tall):
+            at = pl.ds(pl.multiple_of(j * block + m, tall), tall)
+            left = left_ref[first + d, :, at].T
+            rows = pl.ds(pl.multiple_of(i * block + m, tall), tall)
+            for n in range(0, cols, wide):
+                part = jnp.dot(left, right_ref[:, n:n + wide], preferred_element_type=F32)
+                held[rows, n:n + wide] = part.astype(BF16)
+        copy_of(i).start()
+        return carry
+
+    def finish(i, carry):
+        copy_of(i).wait()
+        return carry
+
+    lax.fori_loop(0, n_parts * per, make, 0)
+    lax.fori_loop(0, n_parts * per, finish, 0)
 
 
 def shards(R, C, Z, tokens, cotangent, w_in, b_in, w_out):
@@ -315,25 +346,33 @@
 
     from_col = [shifted(parts[off], "col", C, off) for off in range(1, C)]
     cost = pl.CostEstimate(
-        flops=2 * T * n_feat * n_hid, bytes_accessed=2 * n_feat * n_hid, transcendentals=0
+        flops=T * n_feat * n_hid, bytes_accessed=n_feat * n_hid, transcendentals=0
     )
-    block_f = block_of(n_feat)
-    w_in_grad = pl.pallas_call(
-        grad_kernel,
-        grid=(n_feat // block_f,),
-        in_specs=[
-            pl.BlockSpec((T, block_f), lambda i: (0, i)),
-            pl.BlockSpec((T, n_hid), lambda i: (0, 0)),
-        ],
-        out_specs=pl.BlockSpec((block_f, n_hid), lambda i: (i, 0)),
-        out_shape=shape((n_feat, n_hid), BF16),
-        cost_estimate=cost,
-        name="w_in_grad",
-    )(every_x, grad)
+    def weight_grad(left, right, first, last, name, *held):
+        n_left = left.shape[-1]
+        n_piece = (last - first) * (n_left // block_of(n_left))
+        return pl.pallas_call(
+            functools.partial(grad_kernel, first, last - first),
+            in_specs=[vmem, vmem] + [hbm] * len(held),
+            out_specs=hbm,
+            out_shape=shape((left.shape[0] * n_left, right.shape[1]), BF16),
+            scratch_shapes=[
+                pltpu.VMEM(((last - first) * n_left, right.shape[1]), BF16),
+                dma((n_piece,)),
+            ],
+            input_output_aliases={2: 0} if held else {},
+            compiler_params=pltpu.CompilerParams(vmem_limit_bytes=40 * 1024 * 1024),
+            cost_estimate=cost,
+            name=name,
+        )(left, right, *held)
+
+    w_in_grad = weight_grad(every_x.reshape(1, T, n_feat), grad, 0, 1, "w_in_grad")
+    w_out_grad = weight_grad(act, quarter_g, 0, Z // 2, "w_out_grad")
+    *from_col, w_in_grad, w_out_grad = lax.optimization_barrier((*from_col, w_in_grad, w_out_grad))
     total = parts[0]
     for value in from_col:
         total = total + value.astype(F32)
-    act, total, w_in_grad = lax.optimization_barrier((act, total, w_in_grad))
+    total, w_out_grad = lax.optimization_barrier((total, w_out_grad))
     total = total.reshape(Z, t, n_feat)
 
     def for_depth(off):
@@ -341,20 +380,7 @@
         return lax.dynamic_index_in_dim(total, at, 0, keepdims=False)
 
     from_dep = [shifted(for_depth(off).astype(BF16), "depth", Z, off) for off in range(1, Z)]
-    block_h = block_of(n_hid)
-    per = n_hid // block_h
-    w_out_grad = pl.pallas_call(
-        grad_kernel,
-        grid=(Z, per),
-        in_specs=[
-            pl.BlockSpec((None, T, block_h), lambda d, j: (d, 0, j)),
-            pl.BlockSpec((T, n_d), lambda d, j: (0, 0)),
-        ],
-        out_specs=pl.BlockSpec((block_h, n_d), lambda d, j: (d * per + j, 0)),
-        out_shape=shape((Z * n_hid, n_d), BF16),
-        cost_estimate=cost,
-        name="w_out_grad",
-    )(act, quarter_g)
+    w_out_grad = weight_grad(act, quarter_g, Z // 2, Z, "w_out_grad", w_out_grad)
     input_sum = for_depth(0)
     for value in from_dep:
         input_sum = input_sum + value.astype(F32)

time: 106 us -> 101 us (0.953)
  Pallas kernels: 85 us -> 77.5 us
  local copies, waits for them, and re-layouts: 1.43 us -> 3.84 us
    pallas_call x2 -> x3, Pallas kernels: 25.8 us -> 18.3 us  [weight_grad(): pl.pallas_call(functools.partial(grad_kernel, first, last - first), in_sp...]
    unnamed x2 -> x10, local copies, waits for them, and re-layouts: 0.01 us -> 2.41 us
  transfers between devices with their start and end apart: 6 -> 6, of which waited for: 1 -> 1; matrix products, arithmetic and copies ran while one was open for 1% -> 1% of each run, Pallas kernels for 25% -> 18%
where the time goes in v5:
time: 101 us
  Pallas kernels  77.5 us (77%)
  starting transfers between devices  13 us (13%)
  local copies, waits for them, and re-layouts  3.84 us (4%)
  waiting for transfers between devices  3.57 us (4%)
  other arithmetic  2.15 us (2%)
    pallas_call x1, Pallas kernels, shards(): pl.pallas_call(functools.partial(exchange_kernel, R, C, Z), out_shape=(sh...  59.2 us
    pallas_call x3, Pallas kernels, weight_grad(): pl.pallas_call(functools.partial(grad_kernel, first, last - first), in_sp...  18.3 us
    ppermute x6, starting transfers between devices, shifted(): return lax.ppermute(value, axis, [(i, (i + off) % n) for i in range(n)])  13 us
    ppermute x6, waiting for transfers between devices, shifted(): return lax.ppermute(value, axis, [(i, (i + off) % n) for i in range(n)])  3.57 us
    unnamed x10, local copies, waits for them, and re-layouts  2.41 us
  transfers between devices with their start and end apart: 6, of which 1 were waited for; matrix products, arithmetic and copies ran while one was open for 1% of the time, Pallas kernels for 18%

profile of v5, /device:TPU:0, one launch (start us, length us, event | category | flops | bytes accessed | tf_op | source)
XLA Modules:
  0.0 100.9 jit_solution(17475579543724007441)
XLA Ops:
  0.6 0.8 dynamic_slice.16
  1.4 0.6 reshape.27.b_ref
  2.0 59.2 %exchange.1 = (bf16[128,6144]{1,0:T(8,128)(2,1)}, bf16[128,1536]{1,0:T(8,128)(2,1)}, bf16[128,1536]{1,0:T(8,128)(2,1)}, bf16[4,128,1536]{2,1,0:T(8,128)(2,1)}, f...) custom-call(bf16[8,6144]{1,0:T(8,128)(2,1)} %tok_ref.1, ...), custom_call_target="tpu_custom_call" | custom-call | flops 7247757312 | bytes 37748736 | tf_op jit(solution)/shard_map/exchange/pallas_call | solution.py:301
  61.2 1.2 %collective-permute-start = (bf16[32,6144]{1,0:T(8,128)(2,1)}, bf16[32,6144]{1,0:T(8,128)(2,1)S(1)}, u32[]{:S(2)}, u32[]{:S(2)}) collective-permute-start(bf16[32,6144]{1,0:T(8,128)(2,1)} %get-tuple-element.21), channel_id=1, source_target_pairs={{0,4},{4,8},{8,12},{12,0},{1,5},{5,9},{9,13},{13,1},{2,6},{6,10},{... | collective-permute-start | bytes 1179656 | tf_op jit(solution)/shard_map/ppermute | solution.py:345
  62.4 1.5 %collective-permute-start.1 = (bf16[32,6144]{1,0:T(8,128)(2,1)}, bf16[32,6144]{1,0:T(8,128)(2,1)S(1)}, u32[]{:S(2)}, u32[]{:S(2)}) collective-permute-start(bf16[32,6144]{1,0:T(8,128)(2,1)} %get-tuple-element.22), channel_id=1, source_target_pairs={{0,8},{4,12},{8,0},{12,4},{1,9},{5,13},{9,1},{13,5},{2,10},{6,14},... | collective-permute-start | bytes 1179656 | tf_op jit(solution)/shard_map/ppermute | solution.py:345
  63.9 1.5 %collective-permute-start.2 = (bf16[32,6144]{1,0:T(8,128)(2,1)}, bf16[32,6144]{1,0:T(8,128)(2,1)S(1)}, u32[]{:S(2)}, u32[]{:S(2)}) collective-permute-start(bf16[32,6144]{1,0:T(8,128)(2,1)} %get-tuple-element.23), channel_id=1, source_target_pairs={{0,12},{4,0},{8,4},{12,8},{1,13},{5,1},{9,5},{13,9},{2,14},{6,2},{... | collective-permute-start | bytes 1179656 | tf_op jit(solution)/shard_map/ppermute | solution.py:345
  65.4 1.3 %reduce = f32[1536]{0:T(1024)} reduce(f32[1,1536]{1,0:T(1,128)} %get-tuple-element.34, f32[]{:T(128)} %constant.38), dimensions={0}, to_apply=%get-tuple-element.34.reduce_sub_computation | reduce | bytes 12292 | tf_op jit(solution)/shard_map/exchange/pallas_call | solution.py:301
  66.7 1.4 %copy-done.2 = bf16[128,6144]{1,0:T(8,128)(2,1)S(1)} copy-done((bf16[128,6144]{1,0:T(8,128)(2,1)S(1)}, bf16[128,6144]{1,0:T(8,128)(2,1)}, u32[]{:S(2)}) %copy-start.2) | copy-done | bytes 1572888
  68.1 1.0 copy-done.3
  69.1 8.6 %w_in_grad.1 = bf16[6144,1536]{1,0:T(8,128)(2,1)} custom-call(bf16[1,128,6144]{2,1,0:T(8,128)(2,1)S(1)} %bitcast.19, bf16[128,1536]{1,0:T(8,128)(2,1)S(1)} %copy-done.3), custom_call_target="tpu_custom_call" | custom-call | flops 1207959552 | bytes 9437184 | tf_op jit(solution)/shard_map/w_in_grad/pallas_call | solution.py:354
  77.7 0.0 copy-done
  77.7 4.8 %w_out_grad.2.refs_0_ = bf16[6144,1536]{1,0:T(8,128)(2,1)} custom-call(bf16[4,128,1536]{2,1,0:T(8,128)(2,1)S(1)} %copy-done, bf16[128,1536]{1,0:T(8,128)(2,1)S(1)} %copy-done.1), custom_call_target="tpu_custom_call" | custom-call | flops 1207959552 | bytes 9437184 | tf_op jit(solution)/shard_map/w_out_grad/pallas_call | solution.py:354
  82.6 0.0 collective-permute-done
  82.6 0.0 collective-permute-done.1
  82.6 0.0 collective-permute-done.2
  82.6 0.2 convert_add_fusion
  82.8 4.5 %collective-permute-start.3 = (bf16[8,6144]{1,0:T(8,128)(2,1)S(1)}, bf16[8,6144]{1,0:T(8,128)(2,1)S(1)}, u32[]{:S(2)}, u32[]{:S(2)}) collective-permute-start(bf16[8,6144]{1,0:T(8,128)(2,1)S(1)} %get-tuple-element.36), channel_id=1, source_target_pairs={{0,1},{1,2},{2,3},{3,0},{4,5},{5,6},{6,7},{7,4},{8,9},{9,10},{10,1... | collective-permute-start | bytes 294920 | tf_op jit(solution)/shard_map/ppermute | solution.py:345
  87.4 3.9 %collective-permute-start.5 = (bf16[8,6144]{1,0:T(8,128)(2,1)S(1)}, bf16[8,6144]{1,0:T(8,128)(2,1)S(1)}, u32[]{:S(2)}, u32[]{:S(2)}) collective-permute-start(bf16[8,6144]{1,0:T(8,128)(2,1)S(1)} %get-tuple-element.37), channel_id=1, source_target_pairs={{0,3},{1,0},{2,1},{3,2},{4,7},{5,4},{6,5},{7,6},{8,11},{9,8},{10,9... | collective-permute-start | bytes 294920 | tf_op jit(solution)/shard_map/ppermute | solution.py:345
  91.3 0.5 collective-permute-start.4
  91.8 4.8 %w_out_grad.3 = bf16[6144,1536]{1,0:T(8,128)(2,1)} custom-call(bf16[4,128,1536]{2,1,0:T(8,128)(2,1)S(1)} %copy-done, bf16[128,1536]{1,0:T(8,128)(2,1)S(1)} %copy-done.1, bf16[6144,1536]{1,0:T(8,128)(2,1)} %w_out_grad.2.refs_0_), custom_call_target="tpu_custom_call", output_to_operand_aliasing={{}: (2, {})} | custom-call | flops 1207959552 | bytes 9437184 | tf_op jit(solution)/shard_map/w_out_grad/pallas_call | solution.py:354
  96.6 0.0 collective-permute-done.3
  96.6 0.0 collective-permute-done.5
  96.6 3.6 %collective-permute-done.4 = bf16[8,6144]{1,0:T(8,128)(2,1)S(1)} collective-permute-done((bf16[8,6144]{1,0:T(8,128)(2,1)S(1)}, bf16[8,6144]{1,0:T(8,128)(2,1)S(1)}, u32[]{:S(2)}, u32[]{:S(2)}) %collective-permute-start.4) | collective-permute-done | bytes 98336 | tf_op jit(solution)/shard_map/ppermute | solution.py:345
  100.2 0.7 fusion.2
  (8 shorter events, 0.1 us)
Async XLA Ops:
  61.2 16.5 %copy-start = (bf16[4,128,1536]{2,1,0:T(8,128)(2,1)S(1)}, bf16[4,128,1536]{2,1,0:T(8,128)(2,1)}, u32[]{:S(2)}) copy-start(bf16[4,128,1536]{2,1,0:T(8,128)(2,1)} %get-tuple-element.26.left_ref) | copy-start | bytes 4718596
  61.2 16.5 %copy-start.1 = (bf16[128,1536]{1,0:T(8,128)(2,1)S(1)}, bf16[128,1536]{1,0:T(8,128)(2,1)}, u32[]{:S(2)}) copy-start(bf16[128,1536]{1,0:T(8,128)(2,1)} %get-tuple-element.27.right_ref) | copy-start | bytes 1179652
  61.2 21.3 %collective-permute-start = (bf16[32,6144]{1,0:T(8,128)(2,1)}, bf16[32,6144]{1,0:T(8,128)(2,1)S(1)}, u32[]{:S(2)}, u32[]{:S(2)}) collective-permute-start(bf16[32,6144]{1,0:T(8,128)(2,1)} %get-tuple-element.21), channel_id=1, source_target_pairs={{0,4},{4,8},{8,12},{12,0},{1,5},{5,9},{9,13},{13,1},{2,6},{6,10},{... | collective-permute-start | bytes 1179656 | tf_op jit(solution)/shard_map/ppermute | solution.py:345
  62.4 20.2 %collective-permute-start.1 = (bf16[32,6144]{1,0:T(8,128)(2,1)}, bf16[32,6144]{1,0:T(8,128)(2,1)S(1)}, u32[]{:S(2)}, u32[]{:S(2)}) collective-permute-start(bf16[32,6144]{1,0:T(8,128)(2,1)} %get-tuple-element.22), channel_id=1, source_target_pairs={{0,8},{4,12},{8,0},{12,4},{1,9},{5,13},{9,1},{13,5},{2,10},{6,14},... | collective-permute-start | bytes 1179656 | tf_op jit(solution)/shard_map/ppermute | solution.py:345
  63.9 18.7 %collective-permute-start.2 = (bf16[32,6144]{1,0:T(8,128)(2,1)}, bf16[32,6144]{1,0:T(8,128)(2,1)S(1)}, u32[]{:S(2)}, u32[]{:S(2)}) collective-permute-start(bf16[32,6144]{1,0:T(8,128)(2,1)} %get-tuple-element.23), channel_id=1, source_target_pairs={{0,12},{4,0},{8,4},{12,8},{1,13},{5,1},{9,5},{13,9},{2,14},{6,2},{... | collective-permute-start | bytes 1179656 | tf_op jit(solution)/shard_map/ppermute | solution.py:345
  66.7 1.4 %copy-start.2 = (bf16[128,6144]{1,0:T(8,128)(2,1)S(1)}, bf16[128,6144]{1,0:T(8,128)(2,1)}, u32[]{:S(2)}) copy-start(bf16[128,6144]{1,0:T(8,128)(2,1)} %get-tuple-element.24) | copy-start | bytes 4718596
  68.1 1.0 copy-start.3
  69.1 13.5 %copy-start.4 = (f32[32,6144]{1,0:T(8,128)S(1)}, f32[32,6144]{1,0:T(8,128)}, u32[]{:S(2)}) copy-start(f32[32,6144]{1,0:T(8,128)} %get-tuple-element.20) | copy-start | bytes 2359300
  82.8 13.8 %collective-permute-start.3 = (bf16[8,6144]{1,0:T(8,128)(2,1)S(1)}, bf16[8,6144]{1,0:T(8,128)(2,1)S(1)}, u32[]{:S(2)}, u32[]{:S(2)}) collective-permute-start(bf16[8,6144]{1,0:T(8,128)(2,1)S(1)} %get-tuple-element.36), channel_id=1, source_target_pairs={{0,1},{1,2},{2,3},{3,0},{4,5},{5,6},{6,7},{7,4},{8,9},{9,10},{10,1... | collective-permute-start | bytes 294920 | tf_op jit(solution)/shard_map/ppermute | solution.py:345
  87.4 9.2 %collective-permute-start.5 = (bf16[8,6144]{1,0:T(8,128)(2,1)S(1)}, bf16[8,6144]{1,0:T(8,128)(2,1)S(1)}, u32[]{:S(2)}, u32[]{:S(2)}) collective-permute-start(bf16[8,6144]{1,0:T(8,128)(2,1)S(1)} %get-tuple-element.37), channel_id=1, source_target_pairs={{0,3},{1,0},{2,1},{3,2},{4,7},{5,4},{6,5},{7,6},{8,11},{9,8},{10,9... | collective-permute-start | bytes 294920 | tf_op jit(solution)/shard_map/ppermute | solution.py:345
  91.3 8.9 %collective-permute-start.4 = (bf16[8,6144]{1,0:T(8,128)(2,1)S(1)}, bf16[8,6144]{1,0:T(8,128)(2,1)S(1)}, u32[]{:S(2)}, u32[]{:S(2)}) collective-permute-start(bf16[8,6144]{1,0:T(8,128)(2,1)S(1)} %get-tuple-element.38), channel_id=1, source_target_pairs={{0,2},{1,3},{2,0},{3,1},{4,6},{5,7},{6,4},{7,5},{8,10},{9,11},{10,... | collective-permute-start | bytes 294920 | tf_op jit(solution)/shard_map/ppermute | solution.py:345
